TPU v7x, 32 devices: a whole 2x2x4 slice. The times are simulated.
32 devices in a mesh: win: 2 (over x), seq: 16 (over z, y, core).
Axes of the slice: x: 2, y: 2, z: 4, core: 2. Of those that a mesh axis runs over, the one named last changes fastest.
Arguments:
- code_ids: int32 [4, 2048], P('win', 'seq'), may hold values from 0 to 2047
- conditioning: bfloat16 [4, 2048, 1920], P('win', 'seq'), may hold values from -6 to 6
- code_embedding: bfloat16 [2048, 1920], P(('win', 'seq')), may hold values from -6 to 6
- w_qkv: bfloat16 [1920, 5760], P(('win', 'seq')), may hold values from -0.125 to 0.125
- w_out: bfloat16 [1920, 1920], P(('win', 'seq')), may hold values from -0.375 to 0.375
- w_fc: bfloat16 [1920, 7680], P(('win', 'seq')), may hold values from -0.125 to 0.125
- w_proj: bfloat16 [7680, 1920], P(('win', 'seq')), may hold values from -0.0625 to 0.0625
- norm_gains: bfloat16 [2, 1920], P(None, ('win', 'seq')), may hold values from 0.5 to 1.5
- norm_shifts: bfloat16 [2, 1920], P(None, ('win', 'seq')), may hold values from -3 to 3
- fc_bias: bfloat16 [7680], P(('win', 'seq')), may hold values from -3 to 3
- proj_bias: bfloat16 [1920], P(('win', 'seq')), may hold values from -3 to 3
- cotangent: bfloat16 [4, 2048, 1920], P('win', 'seq'), may hold values from -6 to 6
Outputs:
- layer_out: float32 [4, 2048, 1920], P('win', 'seq')
- grad_conditioning: float32 [4, 2048, 1920], P('win', 'seq')
- grad_embedding: float32 [2048, 1920], P(('win', 'seq'))
- grad_qkv: float32 [1920, 5760], P(('win', 'seq'))
- grad_out: float32 [1920, 1920], P(('win', 'seq'))
- grad_fc: float32 [1920, 7680], P(('win', 'seq'))
- grad_proj: float32 [7680, 1920], P(('win', 'seq'))
- grad_gains: float32 [2, 1920], P(None, ('win', 'seq'))
- grad_shifts: float32 [2, 1920], P(None, ('win', 'seq'))
- grad_fc_bias: float32 [7680], P(('win', 'seq'))
- grad_proj_bias: float32 [1920], P(('win', 'seq'))
All inputs are finite; a program needn't handle non-finite values.
Results may differ from a plain program's by a relative error of at most 0.009.
Values may be sent and summed in bfloat16 or wider, within the bound.
No kernel may reach another device: no remote copies, remote signals or barrier semaphores. Data moves between devices by JAX's collectives and lax.ppermute only.
A program may use at most 320 MiB of HBM per device.

v0:
```python
import math

import jax
import jax.numpy as jnp
from jax import lax
from jax.sharding import PartitionSpec as P

HEADS = 15
HEAD_DIM = 128


EPS = 1e-05


def layer_norm(values, gain_row, shift_row):
    center = values - jnp.mean(values, axis=-1, keepdims=True)
    spread = jnp.mean(center * center, axis=-1, keepdims=True)
    return center * lax.rsqrt(spread + EPS) * gain_row + shift_row


def split_heads(packed_cols):
    shape_in = packed_cols.shape
    return packed_cols.reshape(shape_in[:-1] + (3, HEADS, HEAD_DIM))


def column_scores(queries, key_rows):
    block_rows = queries.shape[1]
    scores = jnp.einsum("wrchd,wschd->wchrs", queries, key_rows, preferred_element_type=jnp.float32)
    scores = scores * (1.0 / math.sqrt(HEAD_DIM))
    causal = lax.broadcasted_iota(jnp.int32, (block_rows, block_rows), 0) >= lax.broadcasted_iota(
        jnp.int32, (block_rows, block_rows), 1
    )
    return jnp.where(causal, scores, -1e30)


def attend(packed_cols):
    split_all = split_heads(packed_cols)
    queries = split_all[:, :, :, 0]
    key_rows = split_all[:, :, :, 1]
    values_all = split_all[:, :, :, 2]
    scores = column_scores(queries, key_rows)
    top_score = jnp.max(scores, axis=-1, keepdims=True)
    expo = jnp.exp(scores - top_score)
    total = jnp.sum(expo, axis=-1, keepdims=True)
    attn_probs = (expo / total).astype(jnp.bfloat16)
    log_total = top_score + jnp.log(total)
    attn_mixed = jnp.einsum(
        "wchrs,wschd->wrchd", attn_probs, values_all, preferred_element_type=jnp.float32
    )
    attn_mixed = attn_mixed.astype(jnp.bfloat16)
    return (attn_mixed.reshape(packed_cols.shape[:-1] + (HEADS * HEAD_DIM,)), log_total)


def attend_back(packed_cols, log_total, grad_cols):
    split_all = split_heads(packed_cols)
    queries = split_all[:, :, :, 0]
    key_rows = split_all[:, :, :, 1]
    values_all = split_all[:, :, :, 2]
    scale_value = 1.0 / math.sqrt(HEAD_DIM)
    probs_full = jnp.exp(column_scores(queries, key_rows) - log_total)
    attn_probs = probs_full.astype(jnp.bfloat16)
    grad_heads = grad_cols.reshape(grad_cols.shape[:-1] + (HEADS, HEAD_DIM))
    grad_values = jnp.einsum(
        "wchrs,wrchd->wschd", attn_probs, grad_heads, preferred_element_type=jnp.float32
    ).astype(jnp.bfloat16)
    grad_probs = jnp.einsum(
        "wrchd,wschd->wchrs", grad_heads, values_all, preferred_element_type=jnp.float32
    )
    inner = jnp.sum(probs_full * grad_probs, axis=-1, keepdims=True)
    grad_scores = (probs_full * (grad_probs - inner)).astype(jnp.bfloat16)
    grad_queries = jnp.einsum(
        "wchrs,wschd->wrchd", grad_scores, key_rows, preferred_element_type=jnp.float32
    )
    grad_queries = (grad_queries * scale_value).astype(jnp.bfloat16)
    grad_keys = jnp.einsum(
        "wchrs,wrchd->wschd", grad_scores, queries, preferred_element_type=jnp.float32
    )
    grad_keys = (grad_keys * scale_value).astype(jnp.bfloat16)
    stacked = jnp.stack([grad_queries, grad_keys, grad_values], axis=3)
    return stacked.reshape(grad_cols.shape[:-1] + (3 * HEADS * HEAD_DIM,))


def gelu_tanh(values):
    return jax.nn.gelu(values, approximate=True)


def shards(
    code_ids,
    conditioning,
    code_embedding,
    w_qkv,
    w_out,
    w_fc,
    w_proj,
    norm_gains,
    norm_shifts,
    fc_bias,
    proj_bias,
    cotangent,
):
    weights_all = (
        lax.all_gather(code_embedding, ("win", "seq"), axis=0, tiled=True),
        lax.all_gather(w_qkv, ("win", "seq"), axis=0, tiled=True),
        lax.all_gather(w_out, ("win", "seq"), axis=0, tiled=True),
        lax.all_gather(w_fc, ("win", "seq"), axis=0, tiled=True),
        lax.all_gather(w_proj, ("win", "seq"), axis=0, tiled=True),
        lax.all_gather(norm_gains, ("win", "seq"), axis=1, tiled=True),
        lax.all_gather(norm_shifts, ("win", "seq"), axis=1, tiled=True),
        lax.all_gather(fc_bias, ("win", "seq"), axis=0, tiled=True),
        lax.all_gather(proj_bias, ("win", "seq"), axis=0, tiled=True),
    )
    (
        embedding,
        qkv_full,
        out_full,
        fc_full,
        proj_full,
        gains_full,
        shifts_full,
        fc_bias_full,
        proj_bias_full,
    ) = weights_all
    gains_f = gains_full.astype(jnp.float32)
    shifts_f = shifts_full.astype(jnp.float32)
    wins_here = code_ids.shape[0]
    block_len = code_ids.shape[1]
    model_width = conditioning.shape[2]
    resid_in = jnp.take(embedding, code_ids, axis=0).astype(jnp.float32) + conditioning.astype(
        jnp.float32
    )
    normed_one = layer_norm(resid_in, gains_f[0], shifts_f[0]).astype(jnp.bfloat16)
    packed_rows = jnp.dot(normed_one, qkv_full, preferred_element_type=jnp.float32).astype(
        jnp.bfloat16
    )
    packed_cols = lax.all_to_all(
        packed_rows[:, None], "seq", split_axis=2, concat_axis=1, tiled=True
    )
    mixed_cols, log_total = attend(packed_cols)
    attn_mixed = lax.all_to_all(mixed_cols, "seq", split_axis=1, concat_axis=2, tiled=True).reshape(
        wins_here, block_len, model_width
    )
    resid_mid = resid_in + jnp.dot(attn_mixed, out_full, preferred_element_type=jnp.float32)
    normed_two = layer_norm(resid_mid, gains_f[1], shifts_f[1]).astype(jnp.bfloat16)
    pre_act = jnp.dot(
        normed_two, fc_full, preferred_element_type=jnp.float32
    ) + fc_bias_full.astype(jnp.float32)
    hidden = gelu_tanh(pre_act).astype(jnp.bfloat16)
    layer_out = (
        resid_mid
        + jnp.dot(hidden, proj_full, preferred_element_type=jnp.float32)
        + proj_bias_full.astype(jnp.float32)
    )
    weights_two = (
        lax.all_gather(code_embedding, ("win", "seq"), axis=0, tiled=True),
        lax.all_gather(w_qkv, ("win", "seq"), axis=0, tiled=True),
        lax.all_gather(w_out, ("win", "seq"), axis=0, tiled=True),
        lax.all_gather(w_fc, ("win", "seq"), axis=0, tiled=True),
        lax.all_gather(w_proj, ("win", "seq"), axis=0, tiled=True),
        lax.all_gather(norm_gains, ("win", "seq"), axis=1, tiled=True),
        lax.all_gather(norm_shifts, ("win", "seq"), axis=1, tiled=True),
        lax.all_gather(fc_bias, ("win", "seq"), axis=0, tiled=True),
        lax.all_gather(proj_bias, ("win", "seq"), axis=0, tiled=True),
    )
    (
        embed_two,
        qkv_two,
        out_two,
        fc_two,
        proj_two,
        gains_two,
        shifts_two,
        fc_bias_two,
        proj_bias_two,
    ) = weights_two
    gains_b = gains_two.astype(jnp.float32)
    shifts_b = shifts_two.astype(jnp.float32)
    grad_proj = jnp.einsum("wtf,wtd->fd", hidden, cotangent, preferred_element_type=jnp.float32)
    grad_proj_bias = jnp.sum(cotangent.astype(jnp.float32), axis=(0, 1))
    grad_hidden = jnp.einsum("wtd,fd->wtf", cotangent, proj_two, preferred_element_type=jnp.float32)
    unused_act, gelu_pull = jax.vjp(gelu_tanh, pre_act)
    grad_pre = gelu_pull(grad_hidden)[0].astype(jnp.bfloat16)
    grad_fc_bias = jnp.sum(grad_pre.astype(jnp.float32), axis=(0, 1))
    grad_fc = jnp.einsum("wtd,wtf->df", normed_two, grad_pre, preferred_element_type=jnp.float32)
    mlp_summed = (
        lax.psum_scatter(grad_fc, ("win", "seq"), scatter_dimension=0, tiled=True),
        lax.psum_scatter(grad_proj, ("win", "seq"), scatter_dimension=0, tiled=True),
        lax.psum_scatter(grad_fc_bias, ("win", "seq"), scatter_dimension=0, tiled=True),
        lax.psum_scatter(grad_proj_bias, ("win", "seq"), scatter_dimension=0, tiled=True),
    )
    grad_normed_two = jnp.einsum(
        "wtf,df->wtd", grad_pre, fc_two, preferred_element_type=jnp.float32
    )
    unused_two, norm_pull_two = jax.vjp(layer_norm, resid_mid, gains_b[1], shifts_b[1])
    grad_mid_norm, grad_gain_two, grad_shift_two = norm_pull_two(grad_normed_two)
    grad_mid = cotangent.astype(jnp.float32) + grad_mid_norm
    grad_branch = grad_mid.astype(jnp.bfloat16)
    grad_out = jnp.einsum(
        "wtd,wte->de", attn_mixed, grad_branch, preferred_element_type=jnp.float32
    )
    grad_mixed = jnp.einsum(
        "wte,de->wtd", grad_branch, out_two, preferred_element_type=jnp.float32
    ).astype(jnp.bfloat16)
    grad_mixed_cols = lax.all_to_all(
        grad_mixed[:, None], "seq", split_axis=2, concat_axis=1, tiled=True
    )
    grad_packed_cols = attend_back(packed_cols, log_total, grad_mixed_cols)
    grad_packed = lax.all_to_all(
        grad_packed_cols, "seq", split_axis=1, concat_axis=2, tiled=True
    ).reshape(wins_here, block_len, 3 * model_width)
    grad_qkv = jnp.einsum(
        "wtd,wte->de", normed_one, grad_packed, preferred_element_type=jnp.float32
    )
    grad_normed_one = jnp.einsum(
        "wte,de->wtd", grad_packed, qkv_two, preferred_element_type=jnp.float32
    )
    unused_one, norm_pull_one = jax.vjp(layer_norm, resid_in, gains_b[0], shifts_b[0])
    grad_in_norm, grad_gain_one, grad_shift_one = norm_pull_one(grad_normed_one)
    grad_conditioning = grad_mid + grad_in_norm
    grad_embedding = jax.ops.segment_sum(
        grad_conditioning.reshape(-1, model_width),
        code_ids.reshape(-1),
        num_segments=embed_two.shape[0],
    )
    grad_gains = jnp.stack([grad_gain_one, grad_gain_two], axis=0)
    grad_shifts = jnp.stack([grad_shift_one, grad_shift_two], axis=0)
    attn_summed = (
        lax.psum_scatter(grad_embedding, ("win", "seq"), scatter_dimension=0, tiled=True),
        lax.psum_scatter(grad_qkv, ("win", "seq"), scatter_dimension=0, tiled=True),
        lax.psum_scatter(grad_out, ("win", "seq"), scatter_dimension=0, tiled=True),
        lax.psum_scatter(grad_gains, ("win", "seq"), scatter_dimension=1, tiled=True),
        lax.psum_scatter(grad_shifts, ("win", "seq"), scatter_dimension=1, tiled=True),
    )
    return (
        layer_out,
        grad_conditioning,
        attn_summed[0],
        attn_summed[1],
        attn_summed[2],
        mlp_summed[0],
        mlp_summed[1],
        attn_summed[3],
        attn_summed[4],
        mlp_summed[2],
        mlp_summed[3],
    )


def solution(mesh):
    return jax.shard_map(
        shards,
        mesh=mesh,
        in_specs=(
            P("win", "seq"),
            P("win", "seq", None),
            P(("win", "seq"), None),
            P(("win", "seq"), None),
            P(("win", "seq"), None),
            P(("win", "seq"), None),
            P(("win", "seq"), None),
            P(None, ("win", "seq")),
            P(None, ("win", "seq")),
            P(("win", "seq")),
            P(("win", "seq")),
            P("win", "seq", None),
        ),
        out_specs=(
            P("win", "seq", None),
            P("win", "seq", None),
            P(("win", "seq"), None),
            P(("win", "seq"), None),
            P(("win", "seq"), None),
            P(("win", "seq"), None),
            P(("win", "seq"), None),
            P(None, ("win", "seq")),
            P(None, ("win", "seq")),
            P(("win", "seq")),
            P(("win", "seq")),
        ),
        check_vma=False,
    )
```

profile of v0, /device:TPU:3, one launch (start us, length us, event | category | flops | bytes accessed | tf_op | source)
XLA Modules:
  0.0 2752.5 jit_solution(15527195626729871085)
XLA Ops:
  10.6 41.2 %all-gather = bf16[32,60,2]{1,2,0:T(2,128)(2,1)S(1)} all-gather(bf16[1,60,2]{1,2,0:T(2,128)(2,1)S(1)} %bitcast.139), channel_id=1, replica_groups=mesh['win'=2,'seq'=16] {'win','seq'}, dimensions={0}, use_global_device_ids=true | all-gather | bytes 7920 | tf_op jit(solution)/shard_map/all_gather | solution.py:107
  52.0 36.5 %all-gather.1 = bf16[32,60,2]{1,2,0:T(2,128)(2,1)S(1)} all-gather(bf16[1,60,2]{1,2,0:T(2,128)(2,1)S(1)} %bitcast.140), channel_id=1, replica_groups=mesh['win'=2,'seq'=16] {'win','seq'}, dimensions={0}, use_global_device_ids=true | all-gather | bytes 7920 | tf_op jit(solution)/shard_map/all_gather | solution.py:108
  88.7 6.7 gather_fusion
  96.5 140.0 %all-gather.15.cloned.1.call-done = bf16[32,60,5760]{2,1,0:T(8,128)(2,1)} async-done(((bf16[1,60,5760]{2,1,0:T(8,128)(2,1)}), bf16[32,60,5760]{2,1,0:T(8,128)(2,1)}) %all-gather.15.cloned.1.call-update) | async-done | bytes 22118416 | tf_op jit(solution)/shard_map/all_gather | solution.py:103
  236.6 22.2 reshape.188
  258.8 12.2 fusion.18
  271.0 4.6 copy.90
  275.6 4.9 all-to-all-start
  280.6 77.3 %all-to-all-done = bf16[2,1,128,5760]{3,0,1,2:T(2,128)(2,1)} async-done(((bf16[2,1,128,5760]{3,0,1,2:T(2,128)(2,1)}), bf16[2,1,128,5760]{3,0,1,2:T(2,128)(2,1)}, u32[]{:S(2)}, u32[]{:S(2)}) %all-to-all-start) | async-done | bytes 2949152 | tf_op jit(solution)/shard_map/all_to_all | solution.py:135
  357.9 2.1 copy.91
  363.3 1.0 copy.97
  364.3 16.8 all-to-all-start.1
  381.7 67.4 %all-reduce.14 = (bf16[1920]{0:T(1024)(128)(2,1)}, bf16[7680]{0:T(1024)(128)(2,1)S(1)}) all-reduce(bf16[1920]{0:T(1024)(128)(2,1)S(1)} %dynamic-update-slice.1, bf16[7680]{0:T(1024)(128)(2,1)S(1)} %dynamic-update-slice), channel_id=1, replica_groups=mesh['win'=2,'seq'=16] {'win','seq'}, use_global_device_ids=true, to_apply=%add.1 | all-reduce | flops 9600 | bytes 38400
  449.1 8.9 reshape.189
  457.9 8.0 fusion.58
  466.0 1.3 copy-done.2
  467.6 85.3 %all-gather.19.cloned.1.call-done = bf16[32,60,7680]{2,1,0:T(8,128)(2,1)} async-done(((bf16[1,60,7680]{2,1,0:T(8,128)(2,1)}), bf16[32,60,7680]{2,1,0:T(8,128)(2,1)}) %all-gather.19.cloned.1.call-update) | async-done | bytes 29491216 | tf_op jit(solution)/shard_map/all_gather | solution.py:105
  552.8 27.4 reshape.190
  580.2 16.5 convolution_add_fusion
  596.7 132.5 %all-gather.13.cloned.1.call-done = bf16[7680,1920]{1,0:T(8,128)(2,1)} async-done(((bf16[240,1920]{1,0:T(8,128)(2,1)}), bf16[7680,1920]{1,0:T(8,128)(2,1)}) %all-gather.13.cloned.1.call-update) | async-done | bytes 29491216 | tf_op jit(solution)/shard_map/all_gather | solution.py:106
  729.2 19.5 convert_reduce_fusion
  748.7 16.9 multiply_reduce_fusion
  765.6 2.2 fusion.55
  768.2 0.9 copy-done.5
  769.2 5.8 fusion.30
  775.0 2.0 copy.99
  776.9 4.3 all-to-all-start.2
  781.3 22.1 all-to-all-done.2
  803.4 1.3 copy.169
  805.9 0.9 multiply_reduce_fusion.3
  810.9 1.8 copy.105
  812.7 6.5 all-to-all-start.3
  819.3 56.3 %all-to-all-done.3 = bf16[2,16,8,5760]{3,2,0,1:T(8,128)(2,1)} async-done(((bf16[2,16,8,5760]{3,2,0,1:T(8,128)(2,1)}), bf16[2,16,8,5760]{3,2,0,1:T(8,128)(2,1)}, u32[]{:S(2)}, u32[]{:S(2)}) %all-to-all-start.3) | async-done | bytes 2949152 | tf_op jit(solution)/shard_map/all_to_all | solution.py:207
  875.6 13.2 fusion.54
  888.9 3.1 multiply_reduce_fusion.1
  892.0 3.1 convert_reduce_fusion.1
  896.4 11.2 scatter_custom_fusion
  907.7 27.1 convolution_bitcast_fusion
  935.9 8.7 convolution_bitcast_fusion.3
  944.6 187.9 %fusion.1 = f32[64,1920]{1,0:T(8,128)S(1)} fusion(f32[1920,1920]{1,0:T(8,128)} %convolution_bitcast_fusion.3), kind=kCustom, calls=%all-reduce-scatter.1 | all-reduce-scatter fusion | flops 3932161 | bytes 15237120
  1133.3 4.4 collective-permute-start.2
  1137.8 24.5 convolution_bitcast_fusion.1
  1162.2 878.9 %fusion.2 = f32[64,7680]{1,0:T(8,128)} fusion(f32[1920,7680]{1,0:T(8,128)} %convolution_bitcast_fusion.1), kind=kCustom, calls=%all-reduce-scatter.2 | all-reduce-scatter fusion | flops 15728641 | bytes 60948480
  2041.1 3.0 slice.44
  2044.1 4.4 collective-permute-start.4
  2048.5 10.4 collective-permute-start.3
  2058.9 2.9 collective-permute-start.5
  2061.8 18.5 convolution_bitcast_fusion.2
  2080.3 573.5 %fusion = f32[64,5760]{1,0:T(8,128)} fusion(f32[1920,5760]{1,0:T(8,128)} %convolution_bitcast_fusion.2), kind=kCustom, calls=%all-reduce-scatter | all-reduce-scatter fusion | flops 11796481 | bytes 45711360
  2653.7 4.4 collective-permute-start
  2658.1 20.9 fusion.25
  2679.1 7.1 concatenate.1
  2686.2 1.2 slice.42
  2687.4 1.9 collective-permute-start.1
  2689.3 1.9 constant_dynamic-slice_fusion.1
  2691.2 21.4 concatenate.2
  2712.7 3.1 constant_dynamic-slice_fusion
  2715.7 1.3 dynamic-slice.6
  2717.0 1.3 dynamic-slice.7
  2718.3 1.3 constant_dynamic-slice_fusion.3
  2719.6 1.3 constant_dynamic-slice_fusion.4
  2720.9 4.8 collective-permute-done.1
  2725.7 17.1 concatenate
  2742.8 2.7 constant_dynamic-slice_fusion.2
  (129 shorter events, 17.9 us)
Async XLA Ops:
  7.2 3.4 copy-start.25
  7.2 44.8 %copy-start.26 = (bf16[2,60]{1,0:T(2,128)(2,1)S(1)}, bf16[2,60]{1,0:T(2,128)(2,1)}, u32[]{:S(2)}) copy-start(bf16[2,60]{1,0:T(2,128)(2,1)} %param.20) | copy-start | bytes 724
  7.2 81.4 %copy-start.24 = (s32[2,128]{1,0:T(2,128)S(1)}, s32[2,128]{1,0:T(2,128)}, u32[]{:S(2)}) copy-start(s32[2,128]{1,0:T(2,128)} %param.12) | copy-start | bytes 3076
  7.2 81.5 %all-gather.11.cloned.1.call-start = ((), (), s32[]{:S(2)}) async-start(), calls=%async_computation.6 | async-start | bytes 8110080 | tf_op jit(solution)/shard_map/all_gather | solution.py:102
  7.9 228.6 %all-gather.15.cloned.1.call-start = ((), (), s32[]{:S(2)}) async-start(), calls=%async_computation.9 | async-start | bytes 24330240 | tf_op jit(solution)/shard_map/all_gather | solution.py:103
  8.7 440.4 %all-gather.17.cloned.1.call-start = ((), (), s32[]{:S(2)}) async-start(), calls=%async_computation.10 | async-start | bytes 8110080 | tf_op jit(solution)/shard_map/all_gather | solution.py:104
  9.4 543.4 %all-gather.19.cloned.1.call-start = ((), (), s32[]{:S(2)}) async-start(), calls=%async_computation.11 | async-start | bytes 32440320 | tf_op jit(solution)/shard_map/all_gather | solution.py:105
  10.0 719.2 %all-gather.13.cloned.1.call-start = ((), (), s32[]{:S(2)}) async-start(), calls=%async_computation.7 | async-start | bytes 30412800 | tf_op jit(solution)/shard_map/all_gather | solution.py:106
  88.7 170.1 %copy-start.19 = (f32[1920]{0:T(1024)}, f32[1920]{0:T(1024)S(1)}, u32[]{:S(2)}) copy-start(f32[1920]{0:T(1024)S(1)} %get-tuple-element.21) | copy-start | bytes 23044
  88.7 6.7 copy-start
  96.5 162.3 %copy-start.21 = (f32[2,128]{1,0:T(2,128)}, f32[2,128]{1,0:T(2,128)S(1)}, u32[]{:S(2)}) copy-start(f32[2,128]{1,0:T(2,128)S(1)} %multiply_reduce_fusion.6) | copy-start | bytes 3076
  275.6 82.3 %all-to-all-start = ((bf16[2,1,128,5760]{3,0,1,2:T(2,128)(2,1)}), bf16[2,1,128,5760]{3,0,1,2:T(2,128)(2,1)}, u32[]{:S(2)}, u32[]{:S(2)}) async-start(bf16[2,1,128,5760]{3,0,1,2:T(2,128)(2,1)} %copy.90), calls=%async_computation | async-start | bytes 5898240 | tf_op jit(solution)/shard_map/all_to_all | solution.py:135
  360.4 1.0 copy-start.13
  360.4 1.3 copy-start.15
  360.4 1.9 copy-start.17
  363.3 17.9 copy-start.27
  363.3 18.1 copy-start.28
  364.3 93.6 %all-to-all-start.1 = ((bf16[2,16,8,1920]{3,2,0,1:T(8,128)(2,1)}), bf16[2,16,8,1920]{3,2,0,1:T(8,128)(2,1)}, u32[]{:S(2)}, u32[]{:S(2)}) async-start(bf16[2,16,8,1920]{3,2,0,1:T(8,128)(2,1)} %copy.97), calls=%async_computation.1 | async-start | bytes 1966080 | tf_op jit(solution)/shard_map/all_to_all | solution.py:139
  466.0 1.3 copy-start.2
  748.7 16.9 copy-start.3
  765.6 2.3 copy-start.8
  767.9 1.3 copy-start.5
  769.2 5.8 copy-start.11
  776.9 26.4 all-to-all-start.2
  804.7 1.2 copy-start.18
  806.8 1.2 copy-start.16
  808.0 1.2 copy-start.14
  812.7 63.0 %copy-start.1 = (bf16[2,128,1920]{2,1,0:T(8,128)(2,1)S(1)}, bf16[2,128,1920]{2,1,0:T(8,128)(2,1)}, u32[]{:S(2)}) copy-start(bf16[2,128,1920]{2,1,0:T(8,128)(2,1)} %param.13) | copy-start | bytes 2949124
  812.7 62.9 %all-to-all-start.3 = ((bf16[2,16,8,5760]{3,2,0,1:T(8,128)(2,1)}), bf16[2,16,8,5760]{3,2,0,1:T(8,128)(2,1)}, u32[]{:S(2)}, u32[]{:S(2)}) async-start(bf16[2,16,8,5760]{3,2,0,1:T(8,128)(2,1)} %copy.105), calls=%async_computation.3 | async-start | bytes 5898240 | tf_op jit(solution)/shard_map/all_to_all | solution.py:207
  819.2 1896.5 %all-reduce.17.cloned.1.call-start = ((), (), s32[]{:S(2)}) async-start(), calls=%async_computation.13 | async-start | bytes 143360
  819.3 69.6 %copy-start.22 = (f32[2,128]{1,0:T(2,128)S(1)}, f32[2,128]{1,0:T(2,128)}, u32[]{:S(2)}) copy-start(f32[2,128]{1,0:T(2,128)} %copy-done.21) | copy-start | bytes 3076
  888.9 3.1 copy-start.6
  888.9 3.1 copy-start.9
  888.9 3.1 copy-start.10
  896.3 1849.2 %reduce-scatter.13.cloned.1.call-start = ((), (), s32[]{:S(2)}) async-start(), calls=%async_computation.8 | async-start | bytes 16220160 | tf_op jit(solution)/shard_map/reduce_scatter | solution.py:227
  907.6 1837.9 %reduce-scatter.15.cloned.1.call-start = ((), (), s32[]{:S(2)}) async-start(), calls=%async_computation.12 | async-start | bytes 60825600
  934.7 0.7 copy-start.23
  934.7 1.2 copy-start.12
  1133.3 1545.7 %collective-permute-start.2 = (f32[64,1920]{1,0:T(8,128)S(1)}, f32[64,1920]{1,0:T(8,128)}, u32[]{:S(2)}, u32[]{:S(2)}) collective-permute-start(f32[64,1920]{1,0:T(8,128)S(1)} %fusion.1), channel_id=1, source_target_pairs={{0,1},{1,2},{2,3},{3,4},{4,5},{5,6},{6,7},{7,8},{8,9},{9,10},{10,1... | collective-permute-start | bytes 1474568
  2041.1 20.7 copy-start.20
  2044.1 647.1 %collective-permute-start.4 = (f32[64,7680]{1,0:T(8,128)}, f32[64,7680]{1,0:T(8,128)}, u32[]{:S(2)}, u32[]{:S(2)}) collective-permute-start(f32[64,7680]{1,0:T(8,128)} %fusion.2), channel_id=1, source_target_pairs={{0,1},{1,2},{2,3},{3,4},{4,5},{5,6},{6,7},{7,8},{8,9},{9,10},{10,1... | collective-permute-start | bytes 5898248
  2048.5 630.5 %collective-permute-start.3 = (f32[60,1920]{1,0:T(8,128)}, f32[60,1920]{1,0:T(8,128)}, u32[]{:S(2)}, u32[]{:S(2)}) collective-permute-start(f32[60,1920]{1,0:T(8,128)} %slice.43), channel_id=1, source_target_pairs={{0,2},{1,3},{2,4},{3,5},{4,6},{5,7},{6,8},{7,9},{8,10},{9,11},{10,... | collective-permute-start | bytes 1382408
  2058.9 632.3 %collective-permute-start.5 = (f32[60,7680]{1,0:T(8,128)}, f32[60,7680]{1,0:T(8,128)}, u32[]{:S(2)}, u32[]{:S(2)}) collective-permute-start(f32[60,7680]{1,0:T(8,128)} %slice.44), channel_id=1, source_target_pairs={{0,2},{1,3},{2,4},{3,5},{4,6},{5,7},{6,8},{7,9},{8,10},{9,11},{10,... | collective-permute-start | bytes 5529608
  2080.3 577.9 %copy-start.4 = (f32[2,128,1920]{2,1,0:T(8,128)S(1)}, f32[2,128,1920]{2,1,0:T(8,128)}, u32[]{:S(2)}) copy-start(f32[2,128,1920]{2,1,0:T(8,128)} %copy-done.2) | copy-start | bytes 5898244
  2653.7 72.0 %collective-permute-start = (f32[64,5760]{1,0:T(8,128)}, f32[64,5760]{1,0:T(8,128)}, u32[]{:S(2)}, u32[]{:S(2)}) collective-permute-start(f32[64,5760]{1,0:T(8,128)} %fusion), channel_id=1, source_target_pairs={{0,1},{1,2},{2,3},{3,4},{4,5},{5,6},{6,7},{7,8},{8,9},{9,10},{10,1... | collective-permute-start | bytes 4423688
  2679.1 7.2 copy-start.7
  2687.4 38.3 %collective-permute-start.1 = (f32[60,5760]{1,0:T(8,128)}, f32[60,5760]{1,0:T(8,128)}, u32[]{:S(2)}, u32[]{:S(2)}) collective-permute-start(f32[60,5760]{1,0:T(8,128)} %slice.42), channel_id=1, source_target_pairs={{0,2},{1,3},{2,4},{3,5},{4,6},{5,7},{6,8},{7,9},{8,10},{9,11},{10,... | collective-permute-start | bytes 4147208
Sparse Core Ops, SparseCore 0:
  10.9 76.9 all-gather.10
  90.8 145.6 all-gather.14
  239.5 111.1 all-gather.16
  353.4 199.3 all-gather.18
  555.6 173.5 all-gather.12
  896.5 134.3 all-reduce.16
  1037.5 241.5 reduce-scatter.12
  1286.1 758.0 reduce-scatter.14
where the time goes:
time: 2770 us; the launch traced here: 2750 us
  blocking collectives  1790 us (65%)
  waiting for transfers between devices  521 us (19%)
  matrix products  196 us (7%)
  local copies, waits for them, and re-layouts  149 us (5%)
  starting transfers between devices  61.3 us (2%)
    unnamed x4, blocking collectives  1710 us
    all_gather x1, waiting for transfers between devices, shards(): lax.all_gather(w_qkv, ('win', 'seq'), axis=0, tiled=True)  140 us
    all_gather x1, waiting for transfers between devices, shards(): lax.all_gather(w_proj, ('win', 'seq'), axis=0, tiled=True)  132 us
    unnamed x78, local copies, waits for them, and re-layouts  128 us
    all_gather x1, waiting for transfers between devices, shards(): lax.all_gather(w_fc, ('win', 'seq'), axis=0, tiled=True)  85.3 us
    all_to_all x1, waiting for transfers between devices, shards(): lax.all_to_all(packed_rows[:, None], 'seq', split_axis=2, concat_axis=1,...  77.3 us
    all_to_all x1, waiting for transfers between devices, shards(): lax.all_to_all(grad_packed_cols, 'seq', split_axis=1, concat_axis=2, tile...  56.3 us
  transfers between devices with their start and end apart: 18, of which 7 were waited for; matrix products, arithmetic and copies ran while one was open for 70% of the time, Pallas kernels for 0%

commit v1 on v0

v1 whole, which is shorter than its diff:
```python
import math

import jax
import jax.numpy as jnp
from jax import lax
from jax.experimental import pallas as pl
from jax.experimental.pallas import tpu as pltpu
from jax.sharding import Mesh, PartitionSpec as P

HEAD_DIM = 128
EPS = 1e-05
F32 = jnp.float32
BF16 = jnp.bfloat16
SEQ = ("h", "l", "y", "c")
ALL = ("x",) + SEQ


def dot(a, b, dims):
    return lax.dot_general(a, b, (dims, ((), ())), preferred_element_type=F32)


def size(axis):
    return lax.axis_size(axis)


def swap(a, axis):
    return lax.ppermute(a, axis, [(0, 1), (1, 0)])


def pick(a, i, dim):
    return lax.dynamic_index_in_dim(a, i, dim, keepdims=False)


def gather_axis(a, axis):
    if size(axis) != 2:
        return lax.all_gather(a, axis, axis=0, tiled=False)
    got = swap(a, axis)
    first = lax.axis_index(axis) == 0
    return jnp.where(first, jnp.stack([a, got]), jnp.stack([got, a]))


def scatter_axis(a, axis, dim):
    if size(axis) != 2:
        return lax.psum_scatter(a.astype(BF16), axis, scatter_dimension=dim, tiled=False).astype(F32)
    me = lax.axis_index(axis)
    got = swap(pick(a, 1 - me, dim).astype(BF16), axis)
    return pick(a, me, dim).astype(F32) + got.astype(F32)


def gather_rows(block):
    both = gather_axis(block, "h")
    a, b = both[:, 0], both[:, 1]
    a = gather_axis(a, "x")
    b = gather_axis(b, "y")
    a = gather_axis(a, "y")
    b = gather_axis(b, "x")
    a = jnp.transpose(a, (1, 2, 0, 3, 4))
    b = jnp.transpose(b, (0, 2, 1, 3, 4))
    return jnp.stack([a, b], axis=2)


def scatter_rows(grad):
    a, b = grad[:, :, 0], grad[:, :, 1]
    a = scatter_axis(a, "y", 2)
    b = scatter_axis(b, "x", 0)
    a = scatter_axis(a, "x", 0)
    b = scatter_axis(b, "y", 1)
    return scatter_axis(jnp.stack([a, b], axis=1), "h", 0)


def trade(a):
    me = lax.axis_index("c")
    got = swap(pick(a, 1 - me, 1), "c")
    mine = pick(a, me, 1)
    first = me == 0
    a = jnp.where(first, jnp.stack([mine, got], 1), jnp.stack([got, mine], 1))
    me = lax.axis_index("l")
    got = swap(pick(a, 1 - me, 0), "l")
    mine = pick(a, me, 0)
    first = me == 0
    return jnp.where(first, jnp.stack([mine, got], 0), jnp.stack([got, mine], 0))


def share(a):
    two = jnp.concatenate([a, swap(a, "l")], axis=0)
    return jnp.concatenate([two, swap(two, "c")], axis=0)


def total(a):
    half = a.shape[0] // 2
    a = a[:half] + swap(a[half:].astype(BF16), "c").astype(F32)
    half = half // 2
    return a[:half] + swap(a[half:].astype(BF16), "l").astype(F32)


def norm_stats(v):
    center = v - jnp.mean(v, axis=-1, keepdims=True)
    inv = lax.rsqrt(jnp.mean(center * center, axis=-1, keepdims=True) + EPS)
    return center * inv, inv


def norm_back(hat, inv, gain, grad):
    g = grad * gain
    back = inv * (g - jnp.mean(g, axis=-1, keepdims=True) - hat * jnp.mean(g * hat, axis=-1, keepdims=True))
    return back, jnp.sum(grad * hat, axis=0), jnp.sum(grad, axis=0)


def probs_of(q, k, cols):
    n = q.shape[0]
    s = dot(q, k, ((1,), (1,))) * (1.0 / math.sqrt(HEAD_DIM))
    t = lax.broadcasted_iota(jnp.int32, (n, n), 0)
    u = lax.broadcasted_iota(jnp.int32, (n, n), 1)
    keep = (lax.rem(t, cols) == lax.rem(u, cols)) & (t >= u)
    s = jnp.where(keep, s, -1e30)
    e = jnp.exp(s - jnp.max(s, axis=-1, keepdims=True))
    return e / jnp.sum(e, axis=-1, keepdims=True)


def head_slices(h, heads):
    return [slice((p * heads + h) * HEAD_DIM, (p * heads + h + 1) * HEAD_DIM) for p in range(3)]


def attend_kernel(heads, cols, packed_ref, out_ref):
    for h in range(heads):
        sq, sk, sv = head_slices(h, heads)
        p = probs_of(packed_ref[:, sq], packed_ref[:, sk], cols)
        out_ref[:, sq] = dot(p.astype(BF16), packed_ref[:, sv], ((1,), (0,))).astype(BF16)


def attend_back_kernel(heads, cols, packed_ref, grad_ref, out_ref):
    scale = 1.0 / math.sqrt(HEAD_DIM)
    for h in range(heads):
        sq, sk, sv = head_slices(h, heads)
        q, k, v, g = packed_ref[:, sq], packed_ref[:, sk], packed_ref[:, sv], grad_ref[:, sq]
        p = probs_of(q, k, cols)
        out_ref[:, sv] = dot(p.astype(BF16), g, ((0,), (0,))).astype(BF16)
        dp = dot(g, v, ((1,), (1,)))
        ds = (p * (dp - jnp.sum(p * dp, axis=-1, keepdims=True))).astype(BF16)
        out_ref[:, sq] = (dot(ds, k, ((1,), (0,))) * scale).astype(BF16)
        out_ref[:, sk] = (dot(ds, q, ((0,), (0,))) * scale).astype(BF16)


def attention(kernel, heads, cols, chunk, out_cols, *arrays):
    tokens = arrays[0].shape[0]
    steps = tokens // chunk
    return pl.pallas_call(
        lambda *refs: kernel(heads, cols, *refs),
        grid=(steps,),
        in_specs=[pl.BlockSpec((chunk, a.shape[1]), lambda i: (i, 0)) for a in arrays],
        out_specs=pl.BlockSpec((chunk, out_cols), lambda i: (i, 0)),
        out_shape=jax.ShapeDtypeStruct((tokens, out_cols), BF16),
        compiler_params=pltpu.CompilerParams(vmem_limit_bytes=32 * 2**20),
        cost_estimate=pl.CostEstimate(flops=tokens * chunk * out_cols * 4, bytes_accessed=tokens * out_cols * 8, transcendentals=0),
    )(*arrays)


def gelu_parts(v):
    k = math.sqrt(2.0 / math.pi)
    th = jnp.tanh(k * (v + 0.044715 * v * v * v))
    value = 0.5 * v * (1.0 + th)
    slope = 0.5 * (1.0 + th) + 0.5 * v * (1.0 - th * th) * k * (1.0 + 3 * 0.044715 * v * v)
    return value, slope


def shards(code_ids, conditioning, code_embedding, w_qkv, w_out, w_fc, w_proj, norm_gains, norm_shifts, fc_bias, proj_bias, cotangent):
    nx, nh, ns = size("x"), size("h"), size("h") * 8
    wins, block_len = code_ids.shape
    cols = block_len // ns
    width = conditioning.shape[2]
    tokens = wins * block_len
    chunk = ns * cols
    rows = w_qkv.shape[0]
    ff_rows = w_proj.shape[0]
    emb_rows = code_embedding.shape[0]
    ff = w_fc.shape[1]
    ff_part = ff // 4
    heads = -(-(width // HEAD_DIM) // 4)
    hw = heads * HEAD_DIM
    pad = 4 * hw - width
    me_l, me_c = lax.axis_index("l"), lax.axis_index("c")
    me_s = lax.axis_index(SEQ)

    small = jnp.concatenate([norm_gains.reshape(-1), norm_shifts.reshape(-1), proj_bias, fc_bias])
    small = lax.all_gather(small, ALL, axis=0, tiled=False)
    gains = jnp.transpose(small[:, : 2 * rows].reshape(-1, 2, rows), (1, 0, 2)).reshape(2, width).astype(F32)
    shifts = jnp.transpose(small[:, 2 * rows : 4 * rows].reshape(-1, 2, rows), (1, 0, 2)).reshape(2, width).astype(F32)
    proj_b = small[:, 4 * rows : 5 * rows].reshape(width).astype(F32)
    fc_b = small[:, 5 * rows :].reshape(nx, nh, 2, 2, 2, 2, ff_rows // 2)
    fc_b = pick(pick(fc_b, me_c, 4), me_l, 2)
    fc_b = jnp.transpose(fc_b, (0, 1, 3, 2, 4)).reshape(ff_part).astype(F32)
    ids = lax.all_gather(code_ids, SEQ, axis=0, tiled=False)
    ids = jnp.transpose(ids, (1, 0, 2)).reshape(wins, ns, ns, cols)

    def to_columns(a):
        return lax.all_to_all(a[:, None], SEQ, split_axis=2, concat_axis=1, tiled=True).reshape(tokens, width)

    def to_rows(a):
        a = a.reshape(wins, ns, cols, width)
        return lax.all_to_all(a, SEQ, split_axis=1, concat_axis=2, tiled=True).reshape(wins, block_len, width)

    cond = to_columns(conditioning)
    cot = to_columns(cotangent)

    def member_cols(w):
        return jnp.transpose(w.reshape(w.shape[0], 2, 2, -1), (1, 2, 0, 3))

    qkv_w = jnp.pad(w_qkv.reshape(rows, 3, width), ((0, 0), (0, 0), (0, pad))).reshape(rows, 3, 4, hw)
    qkv_w = jnp.transpose(qkv_w, (2, 0, 1, 3)).reshape(2, 2, rows, 3 * hw)
    fc_w = w_fc.reshape(rows, nx, nh, 2, 2, 2, 2, ff_rows // 2)
    fc_w = jnp.transpose(fc_w, (3, 5, 0, 1, 2, 6, 4, 7)).reshape(2, 2, rows, ff_part)
    emb_w = gather_rows(code_embedding.reshape(2, emb_rows // 2, width)).reshape(-1, width)
    qkv_w = gather_rows(trade(qkv_w).reshape(2, 2 * rows, 3 * hw)).reshape(width, 3 * hw)
    out_w = gather_rows(trade(member_cols(w_out)).reshape(2, 2 * rows, width // 4)).reshape(width, width // 4)
    out_w = trade(jnp.pad(out_w, ((0, pad), (0, 0))).reshape(2, 2, hw, width // 4))
    out_w = jnp.transpose(out_w, (2, 0, 1, 3)).reshape(hw, width)
    fc_w = gather_rows(trade(fc_w).reshape(2, 2 * rows, ff_part)).reshape(width, ff_part)
    proj_w = gather_rows(w_proj.reshape(2, ff_rows // 2, width)).reshape(ff_part, width)

    s_of = [me_s ^ (dl * 4 + dc) for dc in range(2) for dl in range(2)]
    group_ids = jnp.concatenate([pick(ids, s, 2).reshape(tokens) for s in s_of])
    at = jnp.arange(emb_w.shape[0], dtype=jnp.int32)
    half = emb_rows // 2
    r, at = at % half, at // half
    y, at = at % 2, at // 2
    part, at = at % 2, at // 2
    h, x = at % nh, at // nh
    row_ids = ((((x * nh + h) * 2 + me_l) * 2 + y) * 2 + me_c) * emb_rows + part * half + r
    onehot = (group_ids[:, None] == row_ids[None, :]).astype(BF16)
    emb = total(dot(onehot, emb_w, ((1,), (0,))))
    resid_in = emb + cond.astype(F32)

    hat_one, inv_one = norm_stats(resid_in)
    normed_one = share((hat_one * gains[0] + shifts[0]).astype(BF16))
    packed = dot(normed_one, qkv_w, ((1,), (0,))).astype(BF16)
    mixed = attention(attend_kernel, heads, cols, chunk, hw, packed)
    resid_mid = resid_in + total(dot(mixed, out_w, ((1,), (0,))))

    hat_two, inv_two = norm_stats(resid_mid)
    normed_two = share((hat_two * gains[1] + shifts[1]).astype(BF16))
    pre_act = dot(normed_two, fc_w, ((1,), (0,))) + fc_b
    value, slope = gelu_parts(pre_act)
    hidden = value.astype(BF16)
    layer_out = resid_mid + total(dot(hidden, proj_w, ((1,), (0,)))) + proj_b
    layer_out = to_rows(layer_out.astype(BF16)).astype(F32)

    cot_all = share(cot)
    grad_proj = dot(hidden, cot_all, ((0,), (0,))).reshape(nx, nh, 2, 2, ff_rows // 2, width)
    grad_proj = scatter_rows(grad_proj).reshape(ff_rows, width)
    cot_f = cot.astype(F32)
    grad_pre = (dot(cot_all, proj_w, ((1,), (1,))) * slope).astype(BF16)
    grad_fcb = jnp.sum(grad_pre.astype(F32), axis=0)
    grad_fc = dot(normed_two, grad_pre, ((0,), (0,))).reshape(nx, nh, 2, 2, 2 * rows, ff_part)
    grad_fc = scatter_rows(grad_fc).astype(BF16)
    grad_fc = trade(grad_fc.reshape(2, 2, rows, ff_part))
    grad_fc = grad_fc.reshape(2, 2, rows, nx, nh, 2, 2, ff_rows // 2)
    grad_fc = jnp.transpose(grad_fc, (2, 3, 4, 0, 6, 1, 5, 7)).reshape(rows, ff).astype(F32)
    grad_two = total(dot(grad_pre, fc_w, ((1,), (1,))))
    back, gain_two, shift_two = norm_back(hat_two, inv_two, gains[1], grad_two)
    grad_mid = cot_f + back

    branch = share(grad_mid.astype(BF16))
    grad_out = dot(mixed, branch, ((0,), (0,))).astype(BF16)
    grad_out = jnp.transpose(grad_out.reshape(hw, 2, 2, width // 4), (1, 2, 0, 3))
    grad_out = trade(grad_out).reshape(4 * hw, width // 4)[:width]
    grad_out = scatter_rows(grad_out.reshape(nx, nh, 2, 2, 2 * rows, width // 4)).astype(BF16)
    grad_out = trade(grad_out.reshape(2, 2, rows, width // 4))
    grad_out = jnp.transpose(grad_out, (2, 0, 1, 3)).reshape(rows, width).astype(F32)
    grad_mixed = dot(branch, out_w, ((1,), (1,))).astype(BF16)
    grad_packed = attention(attend_back_kernel, heads, cols, chunk, 3 * hw, packed, grad_mixed)
    grad_qkv = dot(normed_one, grad_packed, ((0,), (0,))).reshape(nx, nh, 2, 2, 2 * rows, 3 * hw)
    grad_qkv = scatter_rows(grad_qkv).astype(BF16)
    grad_qkv = trade(grad_qkv.reshape(2, 2, rows, 3 * hw))
    grad_qkv = jnp.transpose(grad_qkv.reshape(4, rows, 3, hw), (1, 2, 0, 3)).reshape(rows, 3, 4 * hw)
    grad_qkv = grad_qkv[:, :, :width].reshape(rows, 3 * width).astype(F32)
    grad_one = total(dot(grad_packed, qkv_w, ((1,), (1,))))
    back, gain_one, shift_one = norm_back(hat_one, inv_one, gains[0], grad_one)
    grad_cond = (grad_mid + back).astype(BF16)
    grad_cond_all = share(grad_cond)
    grad_cond = to_rows(grad_cond).astype(F32)
    grad_emb = dot(onehot, grad_cond_all, ((0,), (0,))).reshape(nx, nh, 2, 2, emb_rows // 2, width)
    grad_emb = scatter_rows(grad_emb).reshape(emb_rows, width)

    small = jnp.stack([gain_one, gain_two, shift_one, shift_two, jnp.sum(cot_f, axis=0)])
    small = small.reshape(5, nx, nh, 2, 2, 2, rows)
    small = lax.psum_scatter(small, "c", scatter_dimension=5, tiled=False)
    small = lax.psum_scatter(small, "l", scatter_dimension=3, tiled=False)
    small = jnp.transpose(small, (1, 2, 3, 0, 4)).reshape(nx, nh, 2, 5 * rows)
    grad_fcb = jnp.transpose(grad_fcb.reshape(nx, nh, 2, 2, ff_rows // 2), (0, 1, 3, 2, 4)).reshape(nx, nh, 2, ff_rows)
    small = jnp.concatenate([small, grad_fcb], axis=-1)
    small = lax.psum_scatter(small, "y", scatter_dimension=2, tiled=False)
    small = lax.psum_scatter(small, "x", scatter_dimension=0, tiled=False)
    small = lax.psum_scatter(small, "h", scatter_dimension=0, tiled=False)
    return (
        layer_out,
        grad_cond,
        grad_emb,
        grad_qkv,
        grad_out,
        grad_fc,
        grad_proj,
        small[: 2 * rows].reshape(2, rows),
        small[2 * rows : 4 * rows].reshape(2, rows),
        small[5 * rows :],
        small[4 * rows : 5 * rows],
    )


def solution(mesh):
    seq = mesh.shape["seq"]
    fine = Mesh(mesh.devices.reshape(mesh.shape["win"], seq // 8, 2, 2, 2), ALL)
    every = P(ALL, None)
    part = P(None, ALL)
    token = P("x", SEQ, None)
    return jax.shard_map(
        shards,
        mesh=fine,
        in_specs=(P("x", SEQ), token, every, every, every, every, every, part, part, P(ALL), P(ALL), token),
        out_specs=(token, token, every, every, every, every, every, part, part, P(ALL), P(ALL)),
        check_vma=False,
    )
```

time: 2770 us -> 1230 us (0.44)
  blocking collectives: 1790 us -> 128 us
  waiting for transfers between devices: 521 us -> 333 us
  other arithmetic: 24.1 us -> 201 us
  local copies, waits for them, and re-layouts: 149 us -> 265 us
  matrix products: 196 us -> 129 us
  starting transfers between devices: 61.3 us -> 125 us
  Pallas kernels: 0 us -> 28 us
    unnamed x4 -> x6, blocking collectives: 1710 us -> 107 us
    all_gather x5 -> x0, waiting for transfers between devices: 358 us -> none  [the longest x1 140 us: shards(): lax.all_gather(w_qkv, ('win', 'seq'), axis=0, tiled=True)]
    ppermute x0 -> x86, waiting for transfers between devices: none -> 333 us  [swap(): return lax.ppermute(a, axis, [(0, 1), (1, 0)])]
    all_to_all x4, waiting for transfers between devices: 156 us -> 0.01 us  [the longest x2 0.01 us: to_columns(): lax.all_to_all(a[:, None], SEQ, split_axis=2, concat_axis=1, tiled=True)]
    ppermute x0 -> x86, starting transfers between devices: none -> 94.7 us  [swap(): return lax.ppermute(a, axis, [(0, 1), (1, 0)])]
    select_n x0 -> x42, other arithmetic: none -> 91.5 us  [the longest x26 42.2 us: gather_axis(): return jnp.where(first, jnp.stack([a, got]), jnp.stack([got, a]))]
    unnamed x78 -> x270, local copies, waits for them, and re-layouts: 128 us -> 55.3 us
    dot_general x18 -> x14, matrix products: 196 us -> 129 us  [dot(): return lax.dot_general(a, b, (dims, ((), ())), preferred_element_type=F32)]
  transfers between devices with their start and end apart: 18 -> 90, of which waited for: 7 -> 30; matrix products, arithmetic and copies ran while one was open for 70% -> 46% of each run, Pallas kernels for 0% -> 1%
where the time goes in v1:
time: 1230 us; the launch traced here: 1210 us
  waiting for transfers between devices  333 us (27%)
  local copies, waits for them, and re-layouts  265 us (22%)
  other arithmetic  201 us (16%)
  matrix products  129 us (10%)
  blocking collectives  128 us (10%)
  starting transfers between devices  125 us (10%)
  Pallas kernels  28 us (2%)
    ppermute x86, waiting for transfers between devices, swap(): return lax.ppermute(a, axis, [(0, 1), (1, 0)])  333 us
    dot_general x14, matrix products, dot(): return lax.dot_general(a, b, (dims, ((), ())), preferred_element_type=F32)  129 us
    unnamed x6, blocking collectives  107 us
    ppermute x86, starting transfers between devices, swap(): return lax.ppermute(a, axis, [(0, 1), (1, 0)])  94.7 us
    unnamed x270, local copies, waits for them, and re-layouts  55.3 us
    select_n x26, other arithmetic, gather_axis(): return jnp.where(first, jnp.stack([a, got]), jnp.stack([got, a]))  42.2 us
    slice x5, local copies, waits for them, and re-layouts, scatter_rows(): a, b = (grad[:, :, 0], grad[:, :, 1])  34.6 us
    select_n x8, other arithmetic, trade(): a = jnp.where(first, jnp.stack([mine, got], 1), jnp.stack([got, mine], 1))  34.3 us
  transfers between devices with their start and end apart: 90, of which 30 were waited for; matrix products, arithmetic and copies ran while one was open for 46% of the time, Pallas kernels for 1%

profile of v1, /device:TPU:3, one launch (start us, length us, event | category | flops | bytes accessed | tf_op | source)
XLA Modules:
  0.0 1213.2 jit_solution(3501725404587664358)
XLA Ops:
  22.2 6.0 reshape.1278
  37.8 62.7 %all-reduce.2 = bf16[17280]{0:T(1024)(128)(2,1)S(1)} all-reduce(bf16[17280]{0:T(1024)(128)(2,1)S(1)} %dynamic-update-slice), channel_id=3, replica_groups=mesh['x'=2,'h'=2,'l'=2,'y'=2,'c'=2] {'x','h','l','y','c'}, use_global_device_ids=true, to_apply=%add.2 | all-reduce | flops 17280 | bytes 69120
  100.8 21.2 %all-gather.2 = s32[16,2,128]{2,1,0:T(2,128)S(1)} all-gather(s32[1,2,128]{2,1,0:T(2,128)S(1)} %bitcast.620), channel_id=2, replica_groups=mesh['x'=2,'h'=2,'l'=2,'y'=2,'c'=2] {'h','l','y','c'}, dimensions={0}, use_global_device_ids=true | all-gather | bytes 17408 | tf_op jit(solution)/shard_map/all_gather | solution.py:191
  147.5 4.2 broadcast_select_fusion.6
  186.7 5.2 collective-permute-start.5
  209.9 5.3 copy.611
  215.1 33.2 %collective-permute-done.11 = bf16[2,120,1536]{2,1,0:T(8,128)(2,1)} collective-permute-done((bf16[2,120,1536]{2,1,0:T(8,128)(2,1)}, bf16[2,120,1536]{2,1,0:T(8,128)(2,1)}, u32[]{:S(2)}, u32[]{:S(2)}) %collective-permute-start.11) | collective-permute-done | bytes 737312 | tf_op jit(solution)/shard_map/ppermute | solution.py:27
  254.6 7.1 all-to-all-start.2
  270.4 8.5 broadcast_select_fusion.1
  280.6 24.4 %collective-permute-done.6 = bf16[256,1920]{1,0:T(8,128)(2,1)S(1)} collective-permute-done((bf16[256,1920]{1,0:T(8,128)(2,1)S(1)}, bf16[256,1920]{1,0:T(8,128)(2,1)S(1)}, u32[]{:S(2)}, u32[]{:S(2)}) %collective-permute-start.6) | collective-permute-done | bytes 983072 | tf_op jit(solution)/shard_map/ppermute | solution.py:27
  315.4 10.6 collective-permute-done.24
  327.0 20.1 %collective-permute-done.7 = bf16[256,1920]{1,0:T(8,128)(2,1)S(1)} collective-permute-done((bf16[256,1920]{1,0:T(8,128)(2,1)S(1)}, bf16[256,1920]{1,0:T(8,128)(2,1)S(1)}, u32[]{:S(2)}, u32[]{:S(2)}) %collective-permute-start.7) | collective-permute-done | bytes 983072 | tf_op jit(solution)/shard_map/ppermute | solution.py:27
  354.5 7.7 convolution_convert_fusion.refs_0_
  362.3 11.5 shard_map.203
  392.9 12.6 %collective-permute-done.39 = bf16[2,120,1920]{2,1,0:T(8,128)(2,1)S(1)} collective-permute-done((bf16[2,120,1920]{2,1,0:T(8,128)(2,1)}, bf16[2,120,1920]{2,1,0:T(8,128)(2,1)S(1)}, u32[]{:S(2)}, u32[]{:S(2)}) %collective-permute-start.39) | collective-permute-done | bytes 921632 | tf_op jit(solution)/shard_map/ppermute | solution.py:27
  417.4 7.7 collective-permute-done.32
  445.4 12.1 collective-permute-done.43
  459.2 5.3 collective-permute-done.40
  470.0 8.6 collective-permute-done.27
  483.6 4.4 fusion.15
  494.3 10.0 collective-permute-done.33
  518.0 12.0 fusion.51
  530.1 9.4 fusion.138
  545.5 18.0 %convert_reduce_fusion = (f32[1920]{0:T(1024)S(1)}, bf16[1024,1920]{1,0:T(8,128)(2,1)S(1)}) fusion(f32[1024,1920]{1,0:T(8,128)} %copy-done.106, f32[1920]{0:T(1024)S(1)} %reshape.1305, bf16[1920,1920]{1,0:T(8,128)(2,1)} %bitcast.568, bf16[512,1920]{1,0:T(8,128)(2,1)} %collective-permute-done.44, bf16[256,1920]{1,0:T(8,128)(2,1)S(1)} %copy-done.74, ...), kind=kOutput, calls=%fused_computation.9 | convolution fusion | flops 7604795392 | bytes 23116800 | tf_op jit(solution)/shard_map/dot_general | solution.py:19
  563.5 12.8 %fusion.150 = f32[1024,1920]{1,0:T(8,128)S(1)} fusion(bf16[1024,1920]{1,0:T(8,128)(2,1)S(1)} %get-tuple-element.117, bf16[1920,1920]{1,0:T(8,128)(2,1)} %bitcast.573), kind=kOutput, calls=%fused_computation.464 | convolution fusion | flops 7549747200 | bytes 19169280 | tf_op jit(solution)/shard_map/dot_general | solution.py:19
  581.4 16.7 %fusion.49 = f32[1920,1920]{1,0:T(8,128)} fusion(bf16[512,1920]{1,0:T(8,128)(2,1)} %collective-permute-done.44, bf16[256,1920]{1,0:T(8,128)(2,1)S(1)} %copy-done.74, bf16[256,1920]{1,0:T(8,128)(2,1)S(1)} %bitcast.559, f32[1024,1920]{1,0:T(8,128)S(1)} %copy-done.107, f32[1920]{0:T(1024)S(1)} %reshape.1305), kind=kOutput, calls=%fused_computation.165 | convolution fusion | flops 7581204480 | bytes 26549760 | tf_op jit(solution)/shard_map/dot_general | solution.py:19
  598.1 11.3 fusion.144
  617.8 13.3 %fusion.50 = f32[1920,1920]{1,0:T(8,128)} fusion(bf16[1024,1920]{1,0:T(8,128)(2,1)S(1)} %copy-done.109, bf16[512,1920]{1,0:T(8,128)(2,1)} %collective-permute-done.28, bf16[256,1920]{1,0:T(8,128)(2,1)S(1)} %copy-done.77, bf16[256,1920]{1,0:T(8,128)(2,1)S(1)} %copy-done.42), kind=kOutput, calls=%fused_computation.166 | convolution fusion | flops 7561543680 | bytes 22609920 | tf_op jit(solution)/shard_map/dot_general | solution.py:19
  631.0 11.2 fusion.145
  648.9 6.2 collective-permute-done.83
  664.8 33.5 %collective-permute-done.74 = bf16[2,2,120,1920]{3,2,1,0:T(8,128)(2,1)S(1)} collective-permute-done((bf16[2,2,120,1920]{3,2,1,0:T(8,128)(2,1)}, bf16[2,2,120,1920]{3,2,1,0:T(8,128)(2,1)S(1)}, u32[]{:S(2)}, u32[]{:S(2)}) %collective-permute-start.74) | collective-permute-done | bytes 1843232 | tf_op jit(solution)/shard_map/ppermute | solution.py:27
  710.7 7.4 collective-permute-done.84
  726.8 11.7 collective-permute-done.75
  747.5 24.5 %collective-permute-done.46 = bf16[256,1920]{1,0:T(8,128)(2,1)} collective-permute-done((bf16[256,1920]{1,0:T(8,128)(2,1)}, bf16[256,1920]{1,0:T(8,128)(2,1)}, u32[]{:S(2)}, u32[]{:S(2)}) %collective-permute-start.46) | collective-permute-done | bytes 983072 | tf_op jit(solution)/shard_map/ppermute | solution.py:27
  774.3 4.9 fusion.139
  780.3 8.2 all-to-all-start.1
  788.5 18.7 %collective-permute-done.78 = bf16[2,120,1920]{2,0,1:T(2,128)(2,1)} collective-permute-done((bf16[2,120,1920]{2,0,1:T(2,128)(2,1)}, bf16[2,120,1920]{2,0,1:T(2,128)(2,1)}, u32[]{:S(2)}, u32[]{:S(2)}) %collective-permute-start.78) | collective-permute-done | bytes 921632 | tf_op jit(solution)/shard_map/ppermute | solution.py:27
  811.0 4.7 collective-permute-start.79
  817.8 5.3 collective-permute-done.47
  826.0 9.8 collective-permute-start.48
  845.1 8.4 collective-permute-done.80
  857.5 4.7 reshape.1313
  864.4 4.6 fusion.53.refs_1_
  869.0 16.5 %shard_map.204 = bf16[1024,1536]{1,0:T(8,128)(2,1)S(1)} custom-call(bf16[1024,1536]{1,0:T(8,128)(2,1)S(1)} %copy-done.1, bf16[1024,512]{1,0:T(8,128)(2,1)S(1)} %fusion.53.refs_1_), custom_call_target="tpu_custom_call" | custom-call | flops 805306368 | bytes 12582912 | tf_op jit(solution)/shard_map/pallas_call | solution.py:146
  885.5 8.9 fusion.151
  899.7 5.8 convolution_convert_fusion.1
  912.6 11.0 fusion.52
  923.6 8.3 fusion.146
  940.5 8.9 broadcast_select_fusion
  951.1 16.3 %collective-permute-done.58 = bf16[2,2,120,1536]{3,2,1,0:T(8,128)(2,1)S(1)} collective-permute-done((bf16[2,2,120,1536]{3,2,1,0:T(8,128)(2,1)S(1)}, bf16[2,2,120,1536]{3,2,1,0:T(8,128)(2,1)S(1)}, u32[]{:S(2)}, u32[]{:S(2)}) %collective-permute-start.58) | collective-permute-done | bytes 1474592 | tf_op jit(solution)/shard_map/ppermute | solution.py:27
  980.5 5.7 select_n.735
  989.2 11.1 reshape.1293
  1043.9 23.2 %collective-permute-done.71 = bf16[2,120,480]{2,0,1:T(2,128)(2,1)S(1)} collective-permute-done((bf16[2,120,480]{2,0,1:T(2,128)(2,1)S(1)}, bf16[2,120,480]{2,0,1:T(2,128)(2,1)S(1)}, u32[]{:S(2)}, u32[]{:S(2)}) %collective-permute-start.71) | collective-permute-done | bytes 230432 | tf_op jit(solution)/shard_map/ppermute | solution.py:27
  1068.5 4.6 collective-permute-start.72
  1083.3 24.3 %all-reduce.4 = f32[5,2,2,2,2,60]{5,4,3,2,1,0:T(2,128)S(1)} all-reduce(f32[5,2,2,2,2,60]{5,4,3,2,1,0:T(2,128)S(1)} %dynamic-slice_bitcast_fusion.12), channel_id=5, replica_groups=mesh['x'=2,'h'=2,'l'=2,'y'=2,'c'=2] {'l'}, use_global_device_ids=true, to_apply=%region_14.15.clone | all-reduce | flops 4800 | bytes 38400
  1115.5 5.5 all-reduce.5
  1121.7 5.6 all-reduce.6
  1137.2 5.0 all-reduce.7
  1146.5 11.1 all-to-all-start.3
  1169.4 4.2 fusion.7
  1179.0 7.9 collective-permute-done.55
  1191.0 4.4 collective-permute-done.56
  1196.1 4.5 collective-permute-start.57
  1202.0 9.9 collective-permute-done.57
  (717 shorter events, 461.2 us)
Async XLA Ops:
  3.3 120.1 %collective-permute-start.16 = (bf16[2,60,480]{2,0,1:T(2,128)(2,1)}, bf16[2,60,480]{2,0,1:T(2,128)(2,1)}, u32[]{:S(2)}, u32[]{:S(2)}) collective-permute-start(bf16[2,60,480]{2,0,1:T(2,128)(2,1)} %bitcast.544), channel_id=1, source_target_pairs={{0,1},{1,0},{2,3},{3,2},{4,5},{5,4},{6,7},{7,6},{8,9},{9,8},{10,11... | collective-permute-start | bytes 345608 | tf_op jit(solution)/shard_map/ppermute | solution.py:27
  4.0 130.4 %collective-permute-start = (bf16[2,32,1920]{2,1,0:T(8,128)(2,1)}, bf16[2,32,1920]{2,1,0:T(8,128)(2,1)S(1)}, u32[]{:S(2)}, u32[]{:S(2)}) collective-permute-start(bf16[2,32,1920]{2,1,0:T(8,128)(2,1)} %bitcast.611), channel_id=1, source_target_pairs={{0,8},{8,0},{1,9},{9,1},{2,10},{10,2},{3,11},{11,3},{4,12},{12,4},... | collective-permute-start | bytes 737288 | tf_op jit(solution)/shard_map/ppermute | solution.py:27
  8.3 245.4 %all-to-all-start = ((bf16[2,1,128,1920]{3,0,1,2:T(2,128)(2,1)}), bf16[2,1,128,1920]{3,0,1,2:T(2,128)(2,1)S(1)}, u32[]{:S(2)}, u32[]{:S(2)}) async-start(bf16[2,1,128,1920]{3,0,1,2:T(2,128)(2,1)} %bitcast.541), calls=%async_computation | async-start | bytes 1966080 | tf_op jit(solution)/shard_map/all_to_all | solution.py:195
  22.1 114.0 %collective-permute-start.9 = (bf16[2,60,1536]{2,0,1:T(2,128)(2,1)}, bf16[2,60,1536]{2,0,1:T(2,128)(2,1)}, u32[]{:S(2)}, u32[]{:S(2)}) collective-permute-start(bf16[2,60,1536]{2,0,1:T(2,128)(2,1)} %bitcast.543), channel_id=1, source_target_pairs={{0,1},{1,0},{2,3},{3,2},{4,5},{5,4},{6,7},{7,6},{8,9},{9,8},{10,11... | collective-permute-start | bytes 1105928 | tf_op jit(solution)/shard_map/ppermute | solution.py:27
  34.6 109.8 %collective-permute-start.29 = (bf16[2,60,1920]{2,0,1:T(2,128)(2,1)}, bf16[2,60,1920]{2,0,1:T(2,128)(2,1)}, u32[]{:S(2)}, u32[]{:S(2)}) collective-permute-start(bf16[2,60,1920]{2,0,1:T(2,128)(2,1)} %bitcast.542), channel_id=1, source_target_pairs={{0,1},{1,0},{2,3},{3,2},{4,5},{5,4},{6,7},{7,6},{8,9},{9,8},{10,11... | collective-permute-start | bytes 1382408 | tf_op jit(solution)/shard_map/ppermute | solution.py:27
  35.0 171.2 %collective-permute-start.36 = (bf16[2,120,1920]{2,1,0:T(8,128)(2,1)}, bf16[2,120,1920]{2,1,0:T(8,128)(2,1)}, u32[]{:S(2)}, u32[]{:S(2)}) collective-permute-start(bf16[2,120,1920]{2,1,0:T(8,128)(2,1)} %bitcast.113), channel_id=1, source_target_pairs={{0,8},{8,0},{1,9},{9,1},{2,10},{10,2},{3,11},{11,3},{4,12},{12,4},... | collective-permute-start | bytes 2764808 | tf_op jit(solution)/shard_map/ppermute | solution.py:27
  136.1 25.5 %collective-permute-start.1 = (bf16[2,32,1920]{2,1,0:T(8,128)(2,1)}, bf16[2,32,1920]{2,1,0:T(8,128)(2,1)}, u32[]{:S(2)}, u32[]{:S(2)}) collective-permute-start(bf16[2,32,1920]{2,1,0:T(8,128)(2,1)} %get-tuple-element.95), channel_id=1, source_target_pairs={{0,16},{16,0},{1,17},{17,1},{2,18},{18,2},{3,19},{19,3},{4,20},{20... | collective-permute-start | bytes 737288 | tf_op jit(solution)/shard_map/ppermute | solution.py:27
  161.6 31.4 %collective-permute-start.30 = (bf16[2,60,1920]{2,0,1:T(2,128)(2,1)}, bf16[2,60,1920]{2,0,1:T(2,128)(2,1)}, u32[]{:S(2)}, u32[]{:S(2)}) collective-permute-start(bf16[2,60,1920]{2,0,1:T(2,128)(2,1)} %get-tuple-element.77), channel_id=1, source_target_pairs={{0,4},{4,0},{1,5},{5,1},{2,6},{6,2},{3,7},{7,3},{8,12},{12,8},{9,1... | collective-permute-start | bytes 1382408 | tf_op jit(solution)/shard_map/ppermute | solution.py:27
  167.8 32.1 %collective-permute-start.20 = (bf16[2,2,120,480]{3,2,1,0:T(8,128)(2,1)}, bf16[2,2,120,480]{3,2,1,0:T(8,128)(2,1)}, u32[]{:S(2)}, u32[]{:S(2)}) collective-permute-start(bf16[2,2,120,480]{3,2,1,0:T(8,128)(2,1)} %maximum_select_fusion.31), channel_id=1, source_target_pairs={{0,2},{2,0},{1,3},{3,1},{4,6},{6,4},{5,7},{7,5},{8,10},{10,8},{9,1... | collective-permute-start | bytes 1382408 | tf_op jit(solution)/shard_map/ppermute | solution.py:27
  175.9 25.4 %collective-permute-start.22 = (bf16[2,2,120,480]{3,2,1,0:T(8,128)(2,1)}, bf16[2,2,120,480]{3,2,1,0:T(8,128)(2,1)}, u32[]{:S(2)}, u32[]{:S(2)}) collective-permute-start(bf16[2,2,120,480]{3,2,1,0:T(8,128)(2,1)} %maximum_select_fusion.33), channel_id=1, source_target_pairs={{0,16},{16,0},{1,17},{17,1},{2,18},{18,2},{3,19},{19,3},{4,20},{20... | collective-permute-start | bytes 1382408 | tf_op jit(solution)/shard_map/ppermute | solution.py:27
  186.7 79.0 %collective-permute-start.5 = (bf16[512,1920]{1,0:T(8,128)(2,1)}, bf16[512,1920]{1,0:T(8,128)(2,1)}, u32[]{:S(2)}, u32[]{:S(2)}) collective-permute-start(bf16[512,1920]{1,0:T(8,128)(2,1)} %slice.384), channel_id=1, source_target_pairs={{0,1},{1,0},{2,3},{3,2},{4,5},{5,4},{6,7},{7,6},{8,9},{9,8},{10,11... | collective-permute-start | bytes 5898248 | tf_op jit(solution)/shard_map/ppermute | solution.py:27
  192.9 55.4 %collective-permute-start.11 = (bf16[2,120,1536]{2,1,0:T(8,128)(2,1)}, bf16[2,120,1536]{2,1,0:T(8,128)(2,1)}, u32[]{:S(2)}, u32[]{:S(2)}) collective-permute-start(bf16[2,120,1536]{2,1,0:T(8,128)(2,1)} %maximum_select_fusion.25), channel_id=1, source_target_pairs={{0,8},{8,0},{1,9},{9,1},{2,10},{10,2},{3,11},{11,3},{4,12},{12,4},... | collective-permute-start | bytes 2211848 | tf_op jit(solution)/shard_map/ppermute | solution.py:27
  199.9 186.7 %collective-permute-start.31 = (bf16[2,120,1920]{2,1,0:T(8,128)(2,1)}, bf16[2,120,1920]{2,1,0:T(8,128)(2,1)}, u32[]{:S(2)}, u32[]{:S(2)}) collective-permute-start(bf16[2,120,1920]{2,1,0:T(8,128)(2,1)} %maximum_select_fusion.23), channel_id=1, source_target_pairs={{0,8},{8,0},{1,9},{9,1},{2,10},{10,2},{3,11},{11,3},{4,12},{12,4},... | collective-permute-start | bytes 2764808 | tf_op jit(solution)/shard_map/ppermute | solution.py:27
  205.9 57.1 %collective-permute-start.23 = (bf16[2,512,480]{1,2,0:T(8,128)(2,1)}, bf16[2,512,480]{1,2,0:T(8,128)(2,1)}, u32[]{:S(2)}, u32[]{:S(2)}) collective-permute-start(bf16[2,512,480]{1,2,0:T(8,128)(2,1)} %bitcast.599), channel_id=1, source_target_pairs={{0,1},{1,0},{2,3},{3,2},{4,5},{5,4},{6,7},{7,6},{8,9},{9,8},{10,11... | collective-permute-start | bytes 2949128 | tf_op jit(solution)/shard_map/ppermute | solution.py:27
  252.6 53.9 %collective-permute-start.12 = (bf16[2,120,1536]{2,1,0:T(8,128)(2,1)}, bf16[2,120,1536]{2,1,0:T(8,128)(2,1)}, u32[]{:S(2)}, u32[]{:S(2)}) collective-permute-start(bf16[2,120,1536]{2,1,0:T(8,128)(2,1)} %get-tuple-element.63), channel_id=1, source_target_pairs={{0,16},{16,0},{1,17},{17,1},{2,18},{18,2},{3,19},{19,3},{4,20},{20... | collective-permute-start | bytes 2211848 | tf_op jit(solution)/shard_map/ppermute | solution.py:27
  253.1 56.0 %collective-permute-start.14 = (bf16[2,120,1536]{2,1,0:T(8,128)(2,1)}, bf16[2,120,1536]{2,1,0:T(8,128)(2,1)}, u32[]{:S(2)}, u32[]{:S(2)}) collective-permute-start(bf16[2,120,1536]{2,1,0:T(8,128)(2,1)} %get-tuple-element.64), channel_id=1, source_target_pairs={{0,2},{2,0},{1,3},{3,1},{4,6},{6,4},{5,7},{7,5},{8,10},{10,8},{9,1... | collective-permute-start | bytes 2211848 | tf_op jit(solution)/shard_map/ppermute | solution.py:27
  254.6 155.4 %all-to-all-start.2 = ((bf16[2,1,128,1920]{3,0,1,2:T(2,128)(2,1)}), bf16[2,1,128,1920]{3,0,1,2:T(2,128)(2,1)S(1)}, u32[]{:S(2)}, u32[]{:S(2)}) async-start(bf16[2,1,128,1920]{3,0,1,2:T(2,128)(2,1)} %bitcast.579), calls=%async_computation.2 | async-start | bytes 1966080 | tf_op jit(solution)/shard_map/all_to_all | solution.py:195
  269.0 36.0 %collective-permute-start.6 = (bf16[256,1920]{1,0:T(8,128)(2,1)S(1)}, bf16[256,1920]{1,0:T(8,128)(2,1)S(1)}, u32[]{:S(2)}, u32[]{:S(2)}) collective-permute-start(bf16[256,1920]{1,0:T(8,128)(2,1)S(1)} %slice.389), channel_id=1, source_target_pairs={{0,4},{4,0},{1,5},{5,1},{2,6},{6,2},{3,7},{7,3},{8,12},{12,8},{9,1... | collective-permute-start | bytes 2949128 | tf_op jit(solution)/shard_map/ppermute | solution.py:27
  280.4 45.6 %collective-permute-start.24 = (bf16[2,512,480]{1,2,0:T(8,128)(2,1)S(1)}, bf16[2,512,480]{1,2,0:T(8,128)(2,1)S(1)}, u32[]{:S(2)}, u32[]{:S(2)}) collective-permute-start(bf16[2,512,480]{1,2,0:T(8,128)(2,1)S(1)} %bitcast.597), channel_id=1, source_target_pairs={{0,4},{4,0},{1,5},{5,1},{2,6},{6,2},{3,7},{7,3},{8,12},{12,8},{9,1... | collective-permute-start | bytes 2949128 | tf_op jit(solution)/shard_map/ppermute | solution.py:27
  306.5 40.6 %collective-permute-start.7 = (bf16[256,1920]{1,0:T(8,128)(2,1)S(1)}, bf16[256,1920]{1,0:T(8,128)(2,1)S(1)}, u32[]{:S(2)}, u32[]{:S(2)}) collective-permute-start(bf16[256,1920]{1,0:T(8,128)(2,1)S(1)} %add_convert_fusion.2), channel_id=1, source_target_pairs={{0,4},{4,0},{1,5},{5,1},{2,6},{6,2},{3,7},{7,3},{8,12},{12,8},{9,1... | collective-permute-start | bytes 2949128 | tf_op jit(solution)/shard_map/ppermute | solution.py:27
  309.0 43.3 %collective-permute-start.13 = (bf16[2,2,120,1536]{3,2,1,0:T(8,128)(2,1)S(1)}, bf16[2,2,120,1536]{3,2,1,0:T(8,128)(2,1)S(1)}, u32[]{:S(2)}, u32[]{:S(2)}) collective-permute-start(bf16[2,2,120,1536]{3,2,1,0:T(8,128)(2,1)S(1)} %maximum_select_fusion.15), channel_id=1, source_target_pairs={{0,2},{2,0},{1,3},{3,1},{4,6},{6,4},{5,7},{7,5},{8,10},{10,8},{9,1... | collective-permute-start | bytes 4423688 | tf_op jit(solution)/shard_map/ppermute | solution.py:27
  310.8 42.1 %collective-permute-start.15 = (bf16[2,2,120,1536]{3,2,1,0:T(8,128)(2,1)S(1)}, bf16[2,2,120,1536]{3,2,1,0:T(8,128)(2,1)S(1)}, u32[]{:S(2)}, u32[]{:S(2)}) collective-permute-start(bf16[2,2,120,1536]{3,2,1,0:T(8,128)(2,1)S(1)} %maximum_select_fusion.17), channel_id=1, source_target_pairs={{0,16},{16,0},{1,17},{17,1},{2,18},{18,2},{3,19},{19,3},{4,20},{20... | collective-permute-start | bytes 4423688 | tf_op jit(solution)/shard_map/ppermute | solution.py:27
  380.1 32.4 %collective-permute-start.25 = (bf16[512,1920]{1,0:T(8,128)(2,1)}, bf16[512,1920]{1,0:T(8,128)(2,1)}, u32[]{:S(2)}, u32[]{:S(2)}) collective-permute-start(bf16[512,1920]{1,0:T(8,128)(2,1)} %slice.383), channel_id=1, source_target_pairs={{0,1},{1,0},{2,3},{3,2},{4,5},{5,4},{6,7},{7,6},{8,9},{9,8},{10,11... | collective-permute-start | bytes 5898248 | tf_op jit(solution)/shard_map/ppermute | solution.py:27
  391.2 33.8 %collective-permute-start.32 = (bf16[2,120,1920]{2,1,0:T(8,128)(2,1)}, bf16[2,120,1920]{2,1,0:T(8,128)(2,1)}, u32[]{:S(2)}, u32[]{:S(2)}) collective-permute-start(bf16[2,120,1920]{2,1,0:T(8,128)(2,1)} %get-tuple-element.51), channel_id=1, source_target_pairs={{0,16},{16,0},{1,17},{17,1},{2,18},{18,2},{3,19},{19,3},{4,20},{20... | collective-permute-start | bytes 2764808 | tf_op jit(solution)/shard_map/ppermute | solution.py:27
  391.4 36.6 %collective-permute-start.34 = (bf16[2,120,1920]{2,1,0:T(8,128)(2,1)}, bf16[2,120,1920]{2,1,0:T(8,128)(2,1)}, u32[]{:S(2)}, u32[]{:S(2)}) collective-permute-start(bf16[2,120,1920]{2,1,0:T(8,128)(2,1)} %get-tuple-element.52), channel_id=1, source_target_pairs={{0,2},{2,0},{1,3},{3,1},{4,6},{6,4},{5,7},{7,5},{8,10},{10,8},{9,1... | collective-permute-start | bytes 2764808 | tf_op jit(solution)/shard_map/ppermute | solution.py:27
  407.0 57.5 %collective-permute-start.40 = (bf16[2,2,120,1920]{3,2,1,0:T(8,128)(2,1)}, bf16[2,2,120,1920]{3,2,1,0:T(8,128)(2,1)}, u32[]{:S(2)}, u32[]{:S(2)}) collective-permute-start(bf16[2,2,120,1920]{3,2,1,0:T(8,128)(2,1)} %maximum_select_fusion.13), channel_id=1, source_target_pairs={{0,16},{16,0},{1,17},{17,1},{2,18},{18,2},{3,19},{19,3},{4,20},{20... | collective-permute-start | bytes 5529608 | tf_op jit(solution)/shard_map/ppermute | solution.py:27
  409.2 74.4 %collective-permute-start.38 = (bf16[2,2,120,1920]{3,2,1,0:T(8,128)(2,1)}, bf16[2,2,120,1920]{3,2,1,0:T(8,128)(2,1)}, u32[]{:S(2)}, u32[]{:S(2)}) collective-permute-start(bf16[2,2,120,1920]{3,2,1,0:T(8,128)(2,1)} %maximum_select_fusion.12), channel_id=1, source_target_pairs={{0,2},{2,0},{1,3},{3,1},{4,6},{6,4},{5,7},{7,5},{8,10},{10,8},{9,1... | collective-permute-start | bytes 5529608 | tf_op jit(solution)/shard_map/ppermute | solution.py:27
  425.0 32.4 %collective-permute-start.43 = (bf16[256,1920]{1,0:T(8,128)(2,1)S(1)}, bf16[256,1920]{1,0:T(8,128)(2,1)S(1)}, u32[]{:S(2)}, u32[]{:S(2)}) collective-permute-start(bf16[256,1920]{1,0:T(8,128)(2,1)S(1)} %bitcast.556), channel_id=1, source_target_pairs={{0,4},{4,0},{1,5},{5,1},{2,6},{6,2},{3,7},{7,3},{8,12},{12,8},{9,1... | collective-permute-start | bytes 2949128 | tf_op jit(solution)/shard_map/ppermute | solution.py:27
  428.0 76.3 %collective-permute-start.33 = (bf16[2,2,120,1920]{3,2,1,0:T(8,128)(2,1)}, bf16[2,2,120,1920]{3,2,1,0:T(8,128)(2,1)}, u32[]{:S(2)}, u32[]{:S(2)}) collective-permute-start(bf16[2,2,120,1920]{3,2,1,0:T(8,128)(2,1)} %maximum_select_fusion.7), channel_id=1, source_target_pairs={{0,2},{2,0},{1,3},{3,1},{4,6},{6,4},{5,7},{7,5},{8,10},{10,8},{9,1... | collective-permute-start | bytes 5529608 | tf_op jit(solution)/shard_map/ppermute | solution.py:27
  438.2 40.4 %collective-permute-start.27 = (bf16[256,1920]{1,0:T(8,128)(2,1)S(1)}, bf16[256,1920]{1,0:T(8,128)(2,1)S(1)}, u32[]{:S(2)}, u32[]{:S(2)}) collective-permute-start(bf16[256,1920]{1,0:T(8,128)(2,1)S(1)} %add_convert_fusion.1), channel_id=1, source_target_pairs={{0,4},{4,0},{1,5},{5,1},{2,6},{6,2},{3,7},{7,3},{8,12},{12,8},{9,1... | collective-permute-start | bytes 2949128 | tf_op jit(solution)/shard_map/ppermute | solution.py:27
  457.5 50.6 %collective-permute-start.35 = (bf16[2,2,120,1920]{3,2,1,0:T(8,128)(2,1)}, bf16[2,2,120,1920]{3,2,1,0:T(8,128)(2,1)S(1)}, u32[]{:S(2)}, u32[]{:S(2)}) collective-permute-start(bf16[2,2,120,1920]{3,2,1,0:T(8,128)(2,1)} %maximum_select_fusion.9), channel_id=1, source_target_pairs={{0,16},{16,0},{1,17},{17,1},{2,18},{18,2},{3,19},{19,3},{4,20},{20... | collective-permute-start | bytes 5529608 | tf_op jit(solution)/shard_map/ppermute | solution.py:27
  464.5 80.9 %collective-permute-start.44 = (bf16[512,1920]{1,0:T(8,128)(2,1)}, bf16[512,1920]{1,0:T(8,128)(2,1)}, u32[]{:S(2)}, u32[]{:S(2)}) collective-permute-start(bf16[512,1920]{1,0:T(8,128)(2,1)} %pad_maximum_fusion.12), channel_id=1, source_target_pairs={{0,1},{1,0},{2,3},{3,2},{4,5},{5,4},{6,7},{7,6},{8,9},{9,8},{10,11... | collective-permute-start | bytes 5898248 | tf_op jit(solution)/shard_map/ppermute | solution.py:27
  480.1 37.9 %collective-permute-start.28 = (bf16[512,1920]{1,0:T(8,128)(2,1)}, bf16[512,1920]{1,0:T(8,128)(2,1)}, u32[]{:S(2)}, u32[]{:S(2)}) collective-permute-start(bf16[512,1920]{1,0:T(8,128)(2,1)} %pad_maximum_fusion.11), channel_id=1, source_target_pairs={{0,1},{1,0},{2,3},{3,2},{4,5},{5,4},{6,7},{7,6},{8,9},{9,8},{10,11... | collective-permute-start | bytes 5898248 | tf_op jit(solution)/shard_map/ppermute | solution.py:27
  544.2 157.7 %collective-permute-start.41 = (bf16[512,1920]{1,0:T(8,128)(2,1)}, bf16[512,1920]{1,0:T(8,128)(2,1)}, u32[]{:S(2)}, u32[]{:S(2)}) collective-permute-start(bf16[512,1920]{1,0:T(8,128)(2,1)} %slice.382), channel_id=1, source_target_pairs={{0,1},{1,0},{2,3},{3,2},{4,5},{5,4},{6,7},{7,6},{8,9},{9,8},{10,11... | collective-permute-start | bytes 5898248 | tf_op jit(solution)/shard_map/ppermute | solution.py:27
  580.8 125.8 %collective-permute-start.45 = (bf16[512,1920]{1,0:T(8,128)(2,1)}, bf16[512,1920]{1,0:T(8,128)(2,1)}, u32[]{:S(2)}, u32[]{:S(2)}) collective-permute-start(bf16[512,1920]{1,0:T(8,128)(2,1)} %slice.381), channel_id=1, source_target_pairs={{0,1},{1,0},{2,3},{3,2},{4,5},{5,4},{6,7},{7,6},{8,9},{9,8},{10,11... | collective-permute-start | bytes 5898248 | tf_op jit(solution)/shard_map/ppermute | solution.py:27
  613.0 42.1 %collective-permute-start.83 = (bf16[2,2,120,1920]{3,2,1,0:T(8,128)(2,1)}, bf16[2,2,120,1920]{3,2,1,0:T(8,128)(2,1)}, u32[]{:S(2)}, u32[]{:S(2)}) collective-permute-start(bf16[2,2,120,1920]{3,2,1,0:T(8,128)(2,1)} %fusion.30), channel_id=1, source_target_pairs={{0,16},{16,0},{1,17},{17,1},{2,18},{18,2},{3,19},{19,3},{4,20},{20... | collective-permute-start | bytes 5529608 | tf_op jit(solution)/shard_map/ppermute | solution.py:27
  617.1 42.7 %collective-permute-start.81 = (bf16[2,2,120,1920]{3,2,1,0:T(8,128)(2,1)}, bf16[2,2,120,1920]{3,2,1,0:T(8,128)(2,1)S(1)}, u32[]{:S(2)}, u32[]{:S(2)}) collective-permute-start(bf16[2,2,120,1920]{3,2,1,0:T(8,128)(2,1)} %fusion.33), channel_id=1, source_target_pairs={{0,2},{2,0},{1,3},{3,1},{4,6},{6,4},{5,7},{7,5},{8,10},{10,8},{9,1... | collective-permute-start | bytes 5529608 | tf_op jit(solution)/shard_map/ppermute | solution.py:27
  645.7 52.5 %collective-permute-start.74 = (bf16[2,2,120,1920]{3,2,1,0:T(8,128)(2,1)}, bf16[2,2,120,1920]{3,2,1,0:T(8,128)(2,1)S(1)}, u32[]{:S(2)}, u32[]{:S(2)}) collective-permute-start(bf16[2,2,120,1920]{3,2,1,0:T(8,128)(2,1)} %fusion.32), channel_id=1, source_target_pairs={{0,2},{2,0},{1,3},{3,1},{4,6},{6,4},{5,7},{7,5},{8,10},{10,8},{9,1... | collective-permute-start | bytes 5529608 | tf_op jit(solution)/shard_map/ppermute | solution.py:27
  655.1 44.6 %collective-permute-start.76 = (bf16[2,2,120,1920]{3,2,0,1:T(8,128)(2,1)S(1)}, bf16[2,2,120,1920]{3,2,0,1:T(8,128)(2,1)S(1)}, u32[]{:S(2)}, u32[]{:S(2)}) collective-permute-start(bf16[2,2,120,1920]{3,2,0,1:T(8,128)(2,1)S(1)} %fusion.31), channel_id=1, source_target_pairs={{0,16},{16,0},{1,17},{17,1},{2,18},{18,2},{3,19},{19,3},{4,20},{20... | collective-permute-start | bytes 5529608 | tf_op jit(solution)/shard_map/ppermute | solution.py:27
  661.0 57.1 %collective-permute-start.84 = (bf16[2,120,1920]{2,1,0:T(8,128)(2,1)}, bf16[2,120,1920]{2,1,0:T(8,128)(2,1)}, u32[]{:S(2)}, u32[]{:S(2)}) collective-permute-start(bf16[2,120,1920]{2,1,0:T(8,128)(2,1)} %fusion.74), channel_id=1, source_target_pairs={{0,2},{2,0},{1,3},{3,1},{4,6},{6,4},{5,7},{7,5},{8,10},{10,8},{9,1... | collective-permute-start | bytes 2764808 | tf_op jit(solution)/shard_map/ppermute | solution.py:27
  699.7 38.8 %collective-permute-start.75 = (bf16[2,120,1920]{2,1,0:T(8,128)(2,1)S(1)}, bf16[2,120,1920]{2,1,0:T(8,128)(2,1)S(1)}, u32[]{:S(2)}, u32[]{:S(2)}) collective-permute-start(bf16[2,120,1920]{2,1,0:T(8,128)(2,1)S(1)} %fusion.71), channel_id=1, source_target_pairs={{0,16},{16,0},{1,17},{17,1},{2,18},{18,2},{3,19},{19,3},{4,20},{20... | collective-permute-start | bytes 2764808 | tf_op jit(solution)/shard_map/ppermute | solution.py:27
  701.8 38.1 %collective-permute-start.77 = (bf16[2,120,1920]{2,1,0:T(8,128)(2,1)}, bf16[2,120,1920]{2,1,0:T(8,128)(2,1)}, u32[]{:S(2)}, u32[]{:S(2)}) collective-permute-start(bf16[2,120,1920]{2,1,0:T(8,128)(2,1)} %fusion.72), channel_id=1, source_target_pairs={{0,2},{2,0},{1,3},{3,1},{4,6},{6,4},{5,7},{7,5},{8,10},{10,8},{9,1... | collective-permute-start | bytes 2764808 | tf_op jit(solution)/shard_map/ppermute | solution.py:27
  706.6 67.7 %collective-permute-start.42 = (bf16[256,1920]{1,0:T(8,128)(2,1)}, bf16[256,1920]{1,0:T(8,128)(2,1)}, u32[]{:S(2)}, u32[]{:S(2)}) collective-permute-start(bf16[256,1920]{1,0:T(8,128)(2,1)} %slice.387), channel_id=1, source_target_pairs={{0,4},{4,0},{1,5},{5,1},{2,6},{6,2},{3,7},{7,3},{8,12},{12,8},{9,1... | collective-permute-start | bytes 2949128 | tf_op jit(solution)/shard_map/ppermute | solution.py:27
  718.1 53.8 %collective-permute-start.46 = (bf16[256,1920]{1,0:T(8,128)(2,1)}, bf16[256,1920]{1,0:T(8,128)(2,1)}, u32[]{:S(2)}, u32[]{:S(2)}) collective-permute-start(bf16[256,1920]{1,0:T(8,128)(2,1)} %slice.386), channel_id=1, source_target_pairs={{0,4},{4,0},{1,5},{5,1},{2,6},{6,2},{3,7},{7,3},{8,12},{12,8},{9,1... | collective-permute-start | bytes 2949128 | tf_op jit(solution)/shard_map/ppermute | solution.py:27
  723.1 118.3 %collective-permute-start.85 = (bf16[2,120,1920]{2,1,0:T(8,128)(2,1)}, bf16[2,120,1920]{2,1,0:T(8,128)(2,1)}, u32[]{:S(2)}, u32[]{:S(2)}) collective-permute-start(bf16[2,120,1920]{2,1,0:T(8,128)(2,1)} %fusion.75), channel_id=1, source_target_pairs={{0,8},{8,0},{1,9},{9,1},{2,10},{10,2},{3,11},{11,3},{4,12},{12,4},... | collective-permute-start | bytes 2764808 | tf_op jit(solution)/shard_map/ppermute | solution.py:27
  746.0 61.2 %collective-permute-start.78 = (bf16[2,120,1920]{2,0,1:T(2,128)(2,1)}, bf16[2,120,1920]{2,0,1:T(2,128)(2,1)}, u32[]{:S(2)}, u32[]{:S(2)}) collective-permute-start(bf16[2,120,1920]{2,0,1:T(2,128)(2,1)} %fusion.76), channel_id=1, source_target_pairs={{0,8},{8,0},{1,9},{9,1},{2,10},{10,2},{3,11},{11,3},{4,12},{12,4},... | collective-permute-start | bytes 2764808 | tf_op jit(solution)/shard_map/ppermute | solution.py:27
  779.2 43.9 %collective-permute-start.47 = (bf16[256,1920]{1,0:T(8,128)(2,1)}, bf16[256,1920]{1,0:T(8,128)(2,1)}, u32[]{:S(2)}, u32[]{:S(2)}) collective-permute-start(bf16[256,1920]{1,0:T(8,128)(2,1)} %get-tuple-element.25), channel_id=1, source_target_pairs={{0,4},{4,0},{1,5},{5,1},{2,6},{6,2},{3,7},{7,3},{8,12},{12,8},{9,1... | collective-permute-start | bytes 2949128 | tf_op jit(solution)/shard_map/ppermute | solution.py:27
  780.3 81.9 %all-to-all-start.1 = ((bf16[2,16,8,1920]{3,2,0,1:T(8,128)(2,1)}), bf16[2,16,8,1920]{3,2,0,1:T(8,128)(2,1)S(1)}, u32[]{:S(2)}, u32[]{:S(2)}) async-start(bf16[2,16,8,1920]{3,2,0,1:T(8,128)(2,1)} %copy.563), calls=%async_computation.1 | async-start | bytes 1966080 | tf_op jit(solution)/shard_map/all_to_all | solution.py:199
  811.0 24.8 %collective-permute-start.79 = (bf16[2,60,1920]{2,0,1:T(2,128)(2,1)S(1)}, bf16[2,60,1920]{2,0,1:T(2,128)(2,1)S(1)}, u32[]{:S(2)}, u32[]{:S(2)}) collective-permute-start(bf16[2,60,1920]{2,0,1:T(2,128)(2,1)S(1)} %get-tuple-element.75), channel_id=1, source_target_pairs={{0,1},{1,0},{2,3},{3,2},{4,5},{5,4},{6,7},{7,6},{8,9},{9,8},{10,11... | collective-permute-start | bytes 1382408 | tf_op jit(solution)/shard_map/ppermute | solution.py:27
  826.0 37.6 %collective-permute-start.48 = (bf16[512,1920]{1,0:T(8,128)(2,1)}, bf16[512,1920]{1,0:T(8,128)(2,1)}, u32[]{:S(2)}, u32[]{:S(2)}) collective-permute-start(bf16[512,1920]{1,0:T(8,128)(2,1)} %pad_maximum_fusion.13), channel_id=1, source_target_pairs={{0,1},{1,0},{2,3},{3,2},{4,5},{5,4},{6,7},{7,6},{8,9},{9,8},{10,11... | collective-permute-start | bytes 5898248 | tf_op jit(solution)/shard_map/ppermute | solution.py:27
  898.9 73.6 %collective-permute-start.49 = (bf16[512,1920]{1,0:T(8,128)(2,1)}, bf16[512,1920]{1,0:T(8,128)(2,1)}, u32[]{:S(2)}, u32[]{:S(2)}) collective-permute-start(bf16[512,1920]{1,0:T(8,128)(2,1)} %slice.380), channel_id=1, source_target_pairs={{0,1},{1,0},{2,3},{3,2},{4,5},{5,4},{6,7},{7,6},{8,9},{9,8},{10,11... | collective-permute-start | bytes 5898248 | tf_op jit(solution)/shard_map/ppermute | solution.py:27
  912.6 25.1 %collective-permute-start.65 = (bf16[2,512,480]{1,2,0:T(8,128)(2,1)}, bf16[2,512,480]{1,2,0:T(8,128)(2,1)}, u32[]{:S(2)}, u32[]{:S(2)}) collective-permute-start(bf16[2,512,480]{1,2,0:T(8,128)(2,1)} %get-tuple-element.46), channel_id=1, source_target_pairs={{0,1},{1,0},{2,3},{3,2},{4,5},{5,4},{6,7},{7,6},{8,9},{9,8},{10,11... | collective-permute-start | bytes 2949128 | tf_op jit(solution)/shard_map/ppermute | solution.py:27
  933.9 33.4 %collective-permute-start.58 = (bf16[2,2,120,1536]{3,2,1,0:T(8,128)(2,1)S(1)}, bf16[2,2,120,1536]{3,2,1,0:T(8,128)(2,1)S(1)}, u32[]{:S(2)}, u32[]{:S(2)}) collective-permute-start(bf16[2,2,120,1536]{3,2,1,0:T(8,128)(2,1)S(1)} %fusion.55), channel_id=1, source_target_pairs={{0,2},{2,0},{1,3},{3,1},{4,6},{6,4},{5,7},{7,5},{8,10},{10,8},{9,1... | collective-permute-start | bytes 4423688 | tf_op jit(solution)/shard_map/ppermute | solution.py:27
  936.6 33.1 %collective-permute-start.60 = (bf16[2,2,120,1536]{3,2,0,1:T(8,128)(2,1)S(1)}, bf16[2,2,120,1536]{3,2,0,1:T(8,128)(2,1)S(1)}, u32[]{:S(2)}, u32[]{:S(2)}) collective-permute-start(bf16[2,2,120,1536]{3,2,0,1:T(8,128)(2,1)S(1)} %fusion.54), channel_id=1, source_target_pairs={{0,16},{16,0},{1,17},{17,1},{2,18},{18,2},{3,19},{19,3},{4,20},{20... | collective-permute-start | bytes 4423688 | tf_op jit(solution)/shard_map/ppermute | solution.py:27
  968.8 52.7 %collective-permute-start.59 = (bf16[2,120,1536]{2,1,0:T(8,128)(2,1)}, bf16[2,120,1536]{2,1,0:T(8,128)(2,1)}, u32[]{:S(2)}, u32[]{:S(2)}) collective-permute-start(bf16[2,120,1536]{2,1,0:T(8,128)(2,1)} %fusion.77), channel_id=1, source_target_pairs={{0,16},{16,0},{1,17},{17,1},{2,18},{18,2},{3,19},{19,3},{4,20},{20... | collective-permute-start | bytes 2211848 | tf_op jit(solution)/shard_map/ppermute | solution.py:27
  971.3 51.7 %collective-permute-start.61 = (bf16[2,120,1536]{2,1,0:T(8,128)(2,1)}, bf16[2,120,1536]{2,1,0:T(8,128)(2,1)}, u32[]{:S(2)}, u32[]{:S(2)}) collective-permute-start(bf16[2,120,1536]{2,1,0:T(8,128)(2,1)} %fusion.78), channel_id=1, source_target_pairs={{0,2},{2,0},{1,3},{3,1},{4,6},{6,4},{5,7},{7,5},{8,10},{10,8},{9,1... | collective-permute-start | bytes 2211848 | tf_op jit(solution)/shard_map/ppermute | solution.py:27
  975.7 97.6 %collective-permute-start.50 = (bf16[256,1920]{1,0:T(8,128)(2,1)}, bf16[256,1920]{1,0:T(8,128)(2,1)}, u32[]{:S(2)}, u32[]{:S(2)}) collective-permute-start(bf16[256,1920]{1,0:T(8,128)(2,1)} %slice.385), channel_id=1, source_target_pairs={{0,4},{4,0},{1,5},{5,1},{2,6},{6,2},{3,7},{7,3},{8,12},{12,8},{9,1... | collective-permute-start | bytes 2949128 | tf_op jit(solution)/shard_map/ppermute | solution.py:27
  1038.2 28.9 %collective-permute-start.71 = (bf16[2,120,480]{2,0,1:T(2,128)(2,1)S(1)}, bf16[2,120,480]{2,0,1:T(2,128)(2,1)S(1)}, u32[]{:S(2)}, u32[]{:S(2)}) collective-permute-start(bf16[2,120,480]{2,0,1:T(2,128)(2,1)S(1)} %fusion.101), channel_id=1, source_target_pairs={{0,8},{8,0},{1,9},{9,1},{2,10},{10,2},{3,11},{11,3},{4,12},{12,4},... | collective-permute-start | bytes 691208 | tf_op jit(solution)/shard_map/ppermute | solution.py:27
  1043.8 63.8 %collective-permute-start.62 = (bf16[2,120,1536]{2,0,1:T(2,128)(2,1)}, bf16[2,120,1536]{2,0,1:T(2,128)(2,1)}, u32[]{:S(2)}, u32[]{:S(2)}) collective-permute-start(bf16[2,120,1536]{2,0,1:T(2,128)(2,1)} %fusion.79), channel_id=1, source_target_pairs={{0,8},{8,0},{1,9},{9,1},{2,10},{10,2},{3,11},{11,3},{4,12},{12,4},... | collective-permute-start | bytes 2211848 | tf_op jit(solution)/shard_map/ppermute | solution.py:27
  1068.5 59.9 %collective-permute-start.72 = (bf16[2,60,480]{2,0,1:T(2,128)(2,1)}, bf16[2,60,480]{2,0,1:T(2,128)(2,1)S(1)}, u32[]{:S(2)}, u32[]{:S(2)}) collective-permute-start(bf16[2,60,480]{2,0,1:T(2,128)(2,1)} %get-tuple-element.105), channel_id=1, source_target_pairs={{0,1},{1,0},{2,3},{3,2},{4,5},{5,4},{6,7},{7,6},{8,9},{9,8},{10,11... | collective-permute-start | bytes 345608 | tf_op jit(solution)/shard_map/ppermute | solution.py:27
  1078.9 33.1 %collective-permute-start.51 = (bf16[256,1920]{1,0:T(8,128)(2,1)}, bf16[256,1920]{1,0:T(8,128)(2,1)}, u32[]{:S(2)}, u32[]{:S(2)}) collective-permute-start(bf16[256,1920]{1,0:T(8,128)(2,1)} %add_convert_fusion), channel_id=1, source_target_pairs={{0,4},{4,0},{1,5},{5,1},{2,6},{6,2},{3,7},{7,3},{8,12},{12,8},{9,1... | collective-permute-start | bytes 2949128 | tf_op jit(solution)/shard_map/ppermute | solution.py:27
  1114.7 54.7 %collective-permute-start.52 = (bf16[512,1920]{1,0:T(8,128)(2,1)}, bf16[512,1920]{1,0:T(8,128)(2,1)}, u32[]{:S(2)}, u32[]{:S(2)}) collective-permute-start(bf16[512,1920]{1,0:T(8,128)(2,1)} %pad_maximum_fusion.14), channel_id=1, source_target_pairs={{0,1},{1,0},{2,3},{3,2},{4,5},{5,4},{6,7},{7,6},{8,9},{9,8},{10,11... | collective-permute-start | bytes 5898248 | tf_op jit(solution)/shard_map/ppermute | solution.py:27
  1133.7 26.7 %collective-permute-start.64 = (bf16[2,60,1536]{2,0,1:T(2,128)(2,1)}, bf16[2,60,1536]{2,0,1:T(2,128)(2,1)}, u32[]{:S(2)}, u32[]{:S(2)}) collective-permute-start(bf16[2,60,1536]{2,0,1:T(2,128)(2,1)} %get-tuple-element.81), channel_id=1, source_target_pairs={{0,4},{4,0},{1,5},{5,1},{2,6},{6,2},{3,7},{7,3},{8,12},{12,8},{9,1... | collective-permute-start | bytes 1105928 | tf_op jit(solution)/shard_map/ppermute | solution.py:27
  1146.5 54.1 %all-to-all-start.3 = ((bf16[2,16,8,1920]{3,2,0,1:T(8,128)(2,1)}), bf16[2,16,8,1920]{3,2,0,1:T(8,128)(2,1)S(1)}, u32[]{:S(2)}, u32[]{:S(2)}) async-start(bf16[2,16,8,1920]{3,2,0,1:T(8,128)(2,1)} %copy.567), calls=%async_computation.3 | async-start | bytes 1966080 | tf_op jit(solution)/shard_map/all_to_all | solution.py:199
  (148 other events, 2352.2 us)
